TPU v7x, 32 devices: a whole 2x2x4 slice. The times are simulated.
32 devices in a mesh: seq: 8 (over y, x, core), mp: 4 (over z).
Axes of the slice: x: 2, y: 2, z: 4, core: 2. Of those that a mesh axis runs over, the one named last changes fastest.
Arguments:
- normed: bfloat16 [4096, 2048], P('seq'), may hold values from -40 to 40
- out_cotangent: bfloat16 [4096, 2048], P('seq'), may hold values from -6 to 6
- segments: int32 [4096], replicated, may hold values from 0 to 15, never falling along the last dimension, each value on 1 to 512 neighbouring positions
- band_mask: int32 [32, 4], P('seq'), may hold values 0 or 1
- query_weight: bfloat16 [2048, 2048], P(None, 'mp'), may hold values from -0.125 to 0.125
- key_value_weight: bfloat16 [2048, 8, 128], P(None, 'mp'), may hold values from -0.125 to 0.125
- out_weight: bfloat16 [2048, 2048], P('mp'), may hold values from -0.125 to 0.125
Outputs:
- context: bfloat16 [4096, 2048], P('seq', 'mp')
- input_grad: bfloat16 [4096, 2048], P('seq', 'mp')
- key_value_gradient: float32 [2048, 8, 128], P(None, 'mp')
Inputs may be any that keep to these rules, and one draw needn't show every extreme that they name: `segments`: document ids never fall along the sequence; each document holds 1 to 512 tokens, one exactly 512.
All inputs are finite; a program needn't handle non-finite values. No bound on the sum of `band_mask` on one device may be relied on, other than what follows from the above.
Results may differ from a plain program's by a relative error of at most 0.039.
The roundings to bfloat16 on the way count: a program that leaves them out, or rounds other values in their place, can miss the bound.
Values may be sent and summed in bfloat16 or wider, within the bound.
A program may use at most 64 MiB of HBM per device.

v0:
```python
import functools

import jax
import jax.numpy as jnp
from jax import lax
from jax.experimental import pallas as pl
from jax.experimental.pallas import tpu as pltpu
from jax.sharding import PartitionSpec as P

QUERY_HEADS = 32
KEY_VALUE_HEADS = 8
GROUP = QUERY_HEADS // KEY_VALUE_HEADS
HEAD_DIM = 64
BLOCK = 128
MARGIN = 2 * BLOCK
WINDOW = BLOCK + 2 * MARGIN
SCALE = 0.125

MESH = pl.DeviceIdType.MESH
NT = (((1,), (1,)), ((), ()))
f32 = jnp.float32
bf16 = jnp.bfloat16
ANY = pl.BlockSpec(memory_space=pl.ANY)
VMEM = pl.BlockSpec(memory_space=pltpu.VMEM)
SMEM = pl.BlockSpec(memory_space=pltpu.SMEM)


def side_by_side(x):
    return jnp.concatenate([x[h * HEAD_DIM : (h + 1) * HEAD_DIM] for h in range(GROUP)], axis=1)


def stacked(x):
    return jnp.concatenate([x[:, h * BLOCK : (h + 1) * BLOCK] for h in range(GROUP)], axis=0)


def fused_kernel(n, m, sum_seq, x_hbm, oc_hbm, wq_hbm, wkv_hbm, wo_hbm, seg_ref, band_ref,
                 ctx_hbm, ig_ref, kvg_hbm, ctx_ref, raw, wide_raw, x_ref, oc_ref, wq_ref, wkv_ref, wo_ref, q_ref, dc_ref,
                 kvx, kdocs, bias, grad, halo, hin, dq_ref, dkv, part, inb, ls, os, ks, kr, hs, hr, rs, rr,
                 *rest):
    if sum_seq:
        (gt, gsum, sib, quart, got, mine, mix, piece, sib2,
         ss, sr, qs, qr, gs, gr, fs, fr) = rest
    tok, kvc = dkv.shape
    blocks = tok // BLOCK
    kv_heads = kvc // (2 * HEAD_DIM)
    wide = GROUP * HEAD_DIM
    loads = [
        pltpu.make_async_copy(src, dst, ls.at[i])
        for i, (src, dst) in enumerate(
            ((wkv_hbm, raw), (x_hbm, x_ref), (wq_hbm, wq_ref), (oc_hbm, oc_ref), (wo_hbm, wo_ref))
        )
    ]
    for cp in loads:
        cp.start()
    ch = part.shape[2]
    me = lax.axis_index("seq")
    z = lax.axis_index("mp")
    core = me % 2
    sibling = me + 1 - 2 * core
    chip = me // 2
    chips = n // 2

    def seq_dev(i):
        return (i, z)

    def mp_dev(i):
        return (me, i)

    barrier = pltpu.get_barrier_semaphore()
    has_left, has_right = me > 0, me < n - 1
    has_down, has_up = z > 0, z < m - 1

    def greet(dev):
        pl.semaphore_signal(barrier, inc=1, device_id=dev, device_id_type=MESH)

    for there, dev in (
        (has_left, seq_dev(me - 1)),
        (has_right, seq_dev(me + 1)),
        (has_down, mp_dev(z - 1)),
        (has_up, mp_dev(z + 1)),
    ):
        @pl.when(there)
        def _():
            greet(dev)
    if sum_seq:
        for k in range(1, chips):
            greet(seq_dev(((chip + k) % chips) * 2 + core))
    peers = chips - 1 if sum_seq else 0
    for there in (has_left, has_right, has_down, has_up):
        peers = peers + there.astype(jnp.int32)
    pl.semaphore_wait(barrier, peers)

    def remote(src, dst, send, recv, dev):
        return pltpu.make_async_remote_copy(
            src_ref=src, dst_ref=dst, send_sem=send, recv_sem=recv, device_id=dev,
            device_id_type=MESH)

    loads[0].wait()
    span = wide_raw.shape[0] // kv_heads

    @pl.loop(0, wkv_ref.shape[0] // span)
    def _(i):
        wide_raw[...] = raw[pl.ds(pl.multiple_of(i * span * kv_heads, 256), span * kv_heads), :].astype(f32)
        for g in range(kv_heads):
            wkv_ref[pl.ds(pl.multiple_of(i * span, 256), span), g * 128 : (g + 1) * 128] = (
                wide_raw[pl.ds(g, span, stride=kv_heads), :].astype(bf16)
            )

    loads[1].wait()

    @pl.loop(0, tok // 256)
    def _(i):
        r = pl.ds(pl.multiple_of(i * 256, 256), 256)
        ro = pl.ds(pl.multiple_of(i * 256 + MARGIN, 256), 256)
        kvx[ro, :] = jnp.dot(x_ref[r, :], wkv_ref[...], preferred_element_type=f32).astype(bf16)

    before, after = pl.ds(0, MARGIN), pl.ds(MARGIN + tok, MARGIN)
    kv_left = remote(kvx.at[pl.ds(MARGIN, MARGIN)], kvx.at[after], ks.at[0], kr.at[0], seq_dev(me - 1))
    kv_right = remote(kvx.at[pl.ds(tok, MARGIN)], kvx.at[before], ks.at[1], kr.at[1], seq_dev(me + 1))
    pl.when(has_left)(kv_left.start)
    pl.when(has_right)(kv_right.start)

    for kb in range(blocks + 4):
        row = me * blocks + kb - 2
        inside = (row >= 0) & (row < n * blocks)
        docs = seg_ref[pl.ds(jnp.clip(row, 0, n * blocks - 1), 1), :]
        docs = jnp.where(inside, docs, -1)
        kdocs[kb] = jnp.transpose(jnp.broadcast_to(docs, (BLOCK, BLOCK)))

    @pl.loop(0, blocks)
    def _(b):
        qdoc = seg_ref[pl.ds(me * blocks + b, 1), :]
        for o in range(5):
            same = kdocs[b + o] == qdoc
            if o != 2:
                same = same & (band_ref[b, o if o < 2 else o - 1] == 1)
            bias[b, o * BLOCK : (o + 1) * BLOCK, :] = jnp.where(same, 0.0, -1e30).astype(f32)

    grad[...] = jnp.zeros_like(grad)
    loads[2].wait()

    @pl.loop(0, tok // 256)
    def _(i):
        r = pl.ds(pl.multiple_of(i * 256, 256), 256)
        q_ref[r, :] = jnp.dot(x_ref[r, :], wq_ref[...], preferred_element_type=f32).astype(bf16)

    loads[3].wait()
    loads[4].wait()

    @pl.loop(0, tok // 256)
    def _(i):
        r = pl.ds(pl.multiple_of(i * 256, 256), 256)
        dc_ref[r, :] = lax.dot_general(
            oc_ref[r, :], wo_ref[...], NT, preferred_element_type=f32
        ).astype(bf16)

    @pl.when(jnp.logical_not(has_left))
    def _():
        kvx[before, :] = jnp.zeros((MARGIN, kvc), bf16)
        for g in range(kv_heads):
            hin[1, g] = jnp.zeros(hin.shape[2:], bf16)

    @pl.when(jnp.logical_not(has_right))
    def _():
        kvx[after, :] = jnp.zeros((MARGIN, kvc), bf16)
        for g in range(kv_heads):
            hin[0, g] = jnp.zeros(hin.shape[2:], bf16)

    pl.when(has_left)(kv_right.wait_recv)
    pl.when(has_right)(kv_left.wait_recv)

    halos = []
    for g in range(kv_heads):
        cols = slice(g * wide, (g + 1) * wide)
        kcols = slice(g * 2 * HEAD_DIM, (g + 1) * 2 * HEAD_DIM)

        @pl.loop(0, blocks)
        def _(b):
            first = pl.multiple_of(b * BLOCK, BLOCK)
            qt = side_by_side(jnp.transpose(q_ref[pl.ds(first, BLOCK), cols] * SCALE))
            dct = side_by_side(jnp.transpose(dc_ref[pl.ds(first, BLOCK), cols]))
            zero = jnp.zeros_like(qt)
            qz = jnp.concatenate([qt, zero], axis=0)
            dcz = jnp.concatenate([zero, dct], axis=0)
            kv = kvx[pl.ds(first, WINDOW), kcols]
            kvt = jnp.transpose(kv)
            s = jnp.dot(kv, qz, preferred_element_type=f32)
            s = s + jnp.concatenate([bias[b]] * GROUP, axis=1)
            p = jnp.exp(s - jnp.max(s, axis=0, keepdims=True))
            w = p * (1.0 / jnp.sum(p, axis=0, keepdims=True))
            wh = w.astype(bf16)
            ctx = jnp.dot(kvt[HEAD_DIM:], wh, preferred_element_type=f32).astype(bf16)
            delta = jnp.sum(dct.astype(f32) * ctx.astype(f32), axis=0, keepdims=True)
            dp = jnp.dot(kv, dcz, preferred_element_type=f32)
            ds = (w * (dp - delta)).astype(bf16)
            dq = jnp.dot(kvt[:HEAD_DIM], ds, preferred_element_type=f32) * SCALE
            ctx_ref[pl.ds(first, BLOCK), cols] = jnp.transpose(stacked(ctx))
            dq_ref[pl.ds(first, BLOCK), cols] = jnp.transpose(stacked(dq.astype(bf16)))
            d_kv = lax.dot_general(ds, qz, NT, preferred_element_type=f32)
            d_kv = d_kv + lax.dot_general(wh, dcz, NT, preferred_element_type=f32)
            grad[pl.ds(first, WINDOW), kcols] += d_kv

        halo[0, g] = grad[:MARGIN, kcols].astype(bf16)
        halo[1, g] = grad[MARGIN + tok :, kcols].astype(bf16)
        to_left = remote(halo.at[0, g], hin.at[0, g], hs.at[0, g], hr.at[0, g], seq_dev(me - 1))
        to_right = remote(halo.at[1, g], hin.at[1, g], hs.at[1, g], hr.at[1, g], seq_dev(me + 1))
        pl.when(has_left)(to_left.start)
        pl.when(has_right)(to_right.start)
        halos.append((to_left, to_right))

    leave = [pltpu.make_async_copy(ctx_ref, ctx_hbm, os.at[0])]
    leave[0].start()
    zero = jnp.zeros((tok - MARGIN, 2 * HEAD_DIM), f32)
    for g, (to_left, to_right) in enumerate(halos):
        kcols = slice(g * 2 * HEAD_DIM, (g + 1) * 2 * HEAD_DIM)
        pl.when(has_left)(to_right.wait_recv)
        pl.when(has_right)(to_left.wait_recv)
        dkv[:, kcols] = (
            grad[MARGIN : MARGIN + tok, kcols]
            + jnp.concatenate([hin[1, g].astype(f32), zero], axis=0)
            + jnp.concatenate([zero, hin[0, g].astype(f32)], axis=0)
        ).astype(bf16)

    def to_up(c):
        return remote(part.at[c], inb.at[c], rs.at[c], rr.at[c], mp_dev(z + 1))

    def to_down(c):
        slot = jnp.where(c == z - 1, m, c)
        return remote(part.at[c], inb.at[slot], rs.at[c], rr.at[slot], mp_dev(z - 1))

    low = z < m // 2

    @pl.loop(0, m)
    def _(t):
        c = jnp.where(low, m - 1 - t, t)
        rows = pl.ds(pl.multiple_of(c * ch, ch), ch)

        @pl.loop(0, tok // 256)
        def _(i):
            r = pl.ds(pl.multiple_of(i * 256, 256), 256)
            part[c, r, :] = (
                lax.dot_general(dq_ref[r, :], wq_ref[rows, :], NT, preferred_element_type=f32)
                + lax.dot_general(dkv[r, :], wkv_ref[rows, :], NT, preferred_element_type=f32)
            ).astype(bf16)

        @pl.when((z == 0) & (c > z))
        def _():
            to_up(c).start()

        @pl.when((z == m - 1) & (c < z))
        def _():
            to_down(c).start()

    def arrived(slot):
        remote(part.at[0], inb.at[slot], rs.at[0], rr.at[slot], mp_dev(z)).wait_recv()

    def add_in(c, slot):
        arrived(slot)

        @pl.loop(0, tok // 128)
        def _(i):
            r = pl.ds(pl.multiple_of(i * 128, 128), 128)
            part[c, r, :] = (part[c, r, :].astype(f32) + inb[slot, r, :].astype(f32)).astype(bf16)

    inner = (z > 0) & (z < m - 1)

    def up_step(c):
        @pl.when(inner & (c > z))
        def _():
            add_in(c, c)
            to_up(c).start()

    def down_step(c):
        @pl.when(inner & (c < z))
        def _():
            add_in(c, c)
            to_down(c).start()

    def chain_steps(first, last):
        @pl.when(low)
        def _():
            @pl.loop(first, last)
            def _(t):
                up_step(m - 1 - t)
                down_step(t)

        @pl.when(jnp.logical_not(low))
        def _():
            @pl.loop(first, last)
            def _(t):
                down_step(t)
                up_step(m - 1 - t)

    if sum_seq:
        pw = gt.shape[3]
        pr = pw * kv_heads
        dkvt = jnp.transpose(dkv[...])
        for k in range(2):
            half = (1 - core) if k == 0 else core

            @pl.loop(0, chips)
            def _(j):
                cols = pl.ds(pl.multiple_of((2 * j + half) * pw, pw), pw)
                prod = jnp.dot(dkvt, x_ref[:, cols], preferred_element_type=f32)
                if k == 0:
                    gt[0, j] = prod.astype(bf16)
                else:
                    gsum[j] = prod

            if k == 0:
                swap = remote(gt.at[0], sib, ss, sr, seq_dev(sibling))
                swap.start()
        swap.wait_recv()

        def other(k):
            return (chip + k) % chips

        sends = []
        for k in range(1, chips):
            j = other(k)
            gt[1, j] = (gsum[j] + sib[j].astype(f32)).astype(bf16)
            cp = remote(gt.at[1, j], quart.at[k], qs.at[k], qr.at[k], seq_dev(j * 2 + core))
            cp.start()
            sends.append(cp)
        mine[...] = gsum[chip] + sib[chip].astype(f32)
        swap.wait_send()

        @pl.when(low)
        def _():
            up_step(m - 1)

        @pl.when(jnp.logical_not(low))
        def _():
            down_step(0)

        for cp in sends:
            cp.wait_recv()
        for k in range(1, chips):
            mine[...] += quart[k].astype(f32)
        for cp in sends:
            cp.wait_send()
        done = jnp.transpose(mine[...])
        for g in range(kv_heads):
            kcols = slice(g * 2 * HEAD_DIM, (g + 1) * 2 * HEAD_DIM)
            mix[pl.ds(g, pw, stride=kv_heads), :] = done[:, kcols]
        piece[...] = mix[...].astype(bf16)
        sends = []
        for k in range(1, chips):
            cp = remote(piece, got.at[k], gs.at[k], gr.at[k], seq_dev(other(k) * 2 + core))
            cp.start()
            sends.append(cp)

        @pl.when(low)
        def _():
            down_step(0)

        @pl.when(jnp.logical_not(low))
        def _():
            up_step(m - 1)

        chain_steps(1, m)
        got[0] = piece[...]
        for cp in sends:
            cp.wait()
        swap = remote(got, sib2, fs, fr, seq_dev(sibling))
        swap.start()
        for k in range(chips):
            src = (chip + chips - k) % chips
            rows = pl.ds(pl.multiple_of((2 * src + core) * pr, pr), pr)
            leave.append(pltpu.make_async_copy(got.at[k], kvg_hbm.at[rows], os.at[1 + k]))
            leave[-1].start()
        swap.wait_recv()
        for k in range(chips):
            src = (chip + chips - k) % chips
            rows = pl.ds(pl.multiple_of((2 * src + 1 - core) * pr, pr), pr)
            leave.append(pltpu.make_async_copy(sib2.at[k], kvg_hbm.at[rows], os.at[1 + chips + k]))
            leave[-1].start()
        swap.wait_send()
    else:
        leave.append(pltpu.make_async_copy(dkv, kvg_hbm, os.at[1]))
        leave[1].start()
        chain_steps(0, m)

    @pl.when(has_down)
    def _():
        arrived(z)

    @pl.when(jnp.logical_not(has_down))
    def _():
        inb[0] = jnp.zeros(inb.shape[1:], bf16)

    @pl.when(has_up)
    def _():
        arrived(m)

    @pl.when(jnp.logical_not(has_up))
    def _():
        inb[m] = jnp.zeros(inb.shape[1:], bf16)

    @pl.loop(0, tok // 128)
    def _(i):
        r = pl.ds(pl.multiple_of(i * 128, 128), 128)
        ig_ref[r, :] = (
            part[z, r, :].astype(f32) + inb[z, r, :].astype(f32) + inb[m, r, :].astype(f32)
        ).astype(bf16)

    @pl.loop(0, m)
    def _(c):
        @pl.when(c > z)
        def _():
            to_up(c).wait_send()

        @pl.when(c < z)
        def _():
            to_down(c).wait_send()

    for cp in leave:
        cp.wait()
    pl.when(has_left)(kv_left.wait_send)
    pl.when(has_right)(kv_right.wait_send)
    for to_left, to_right in halos:
        pl.when(has_left)(to_left.wait_send)
        pl.when(has_right)(to_right.wait_send)


def write_kernel(ctx_hbm, ig_hbm, kvg_hbm, ctx_out, ig_out, kvg_out, half, full, ctx_mid, ig_mid, ins, outs):
    pieces, rows = half.shape[0], half.shape[1]
    loads, stores = [], []
    for i in range(pieces):
        loads.append(pltpu.make_async_copy(kvg_hbm.at[pl.ds(i * rows, rows)], half.at[i], ins.at[i]))
        stores.append(pltpu.make_async_copy(full.at[i], kvg_out.at[pl.ds(i * rows, rows)], outs.at[i]))
        loads[i].start()
    for i, (src, mid, dst) in enumerate(((ctx_hbm, ctx_mid, ctx_out), (ig_hbm, ig_mid, ig_out))):
        loads.append(pltpu.make_async_copy(src, mid, ins.at[pieces + i]))
        stores.append(pltpu.make_async_copy(mid, dst, outs.at[pieces + i]))
        loads[-1].start()
    for i in range(pieces):
        loads[i].wait()
        full[i] = half[i].astype(f32)
        stores[i].start()
    for i in range(pieces, pieces + 2):
        loads[i].wait()
        stores[i].start()
    for cp in stores:
        cp.wait()


def written(*arrays):
    pieces = 4
    rows, lanes = arrays[2].shape[0] // pieces, arrays[2].shape[1]
    return pl.pallas_call(
        write_kernel,
        out_shape=[
            jax.ShapeDtypeStruct(a.shape, t) for a, t in zip(arrays, (bf16, bf16, f32))
        ],
        in_specs=[ANY] * 3,
        out_specs=[ANY] * 3,
        scratch_shapes=[
            pltpu.VMEM((pieces, rows, lanes), bf16),
            pltpu.VMEM((pieces, rows, lanes), f32),
            pltpu.VMEM(arrays[0].shape, bf16),
            pltpu.VMEM(arrays[1].shape, bf16),
            pltpu.SemaphoreType.DMA((pieces + 2,)),
            pltpu.SemaphoreType.DMA((pieces + 2,)),
        ],
        compiler_params=pltpu.CompilerParams(vmem_limit_bytes=60 * 2**20),
        name="write",
    )(*arrays)


def local(n, m, normed, out_cotangent, segments, band_mask, query_weight, key_value_weight, out_weight):
    tok, width = normed.shape
    qc = query_weight.shape[1]
    kv_heads = key_value_weight.shape[1]
    pair = 2 * HEAD_DIM
    kvc = kv_heads * pair
    wkv = key_value_weight.reshape(width * kv_heads, pair)
    blocks = tok // BLOCK
    ch = width // m
    pw = width // n
    sum_seq = n % 2 == 0 and n * 128 <= width and width % (n * 128) == 0
    chips = n // 2
    dma = pltpu.SemaphoreType.DMA
    vmem = pltpu.VMEM
    scratch = [
        vmem((tok, qc), bf16),
        vmem((width * kv_heads, pair), bf16),
        vmem((256 * kv_heads, pair), f32),
        vmem((tok, width), bf16),
        vmem((tok, width), bf16),
        vmem((width, qc), bf16),
        vmem((width, kvc), bf16),
        vmem((qc, width), bf16),
        vmem((tok, qc), bf16),
        vmem((tok, qc), bf16),
        vmem((tok + 2 * MARGIN, kvc), bf16),
        vmem((blocks + 4, BLOCK, BLOCK), jnp.int32),
        vmem((blocks, WINDOW, BLOCK), f32),
        vmem((tok + 2 * MARGIN, kvc), f32),
        vmem((2, kv_heads, MARGIN, pair), bf16),
        vmem((2, kv_heads, MARGIN, pair), bf16),
        vmem((tok, qc), bf16),
        vmem((tok, kvc), bf16),
        vmem((m, tok, ch), bf16),
        vmem((m + 1, tok, ch), bf16),
        dma((5,)),
        dma((1 + n,)),
        dma((2,)),
        dma((2,)),
        dma((2, kv_heads)),
        dma((2, kv_heads)),
        dma((m,)),
        dma((m + 1,)),
    ]
    if sum_seq:
        kvg_shape = (width * kv_heads, pair)
        scratch += [
            vmem((2, chips, kvc, pw), bf16),
            vmem((chips, kvc, pw), f32),
            vmem((chips, kvc, pw), bf16),
            vmem((chips, kvc, pw), bf16),
            vmem((chips, pw * kv_heads, pair), bf16),
            vmem((kvc, pw), f32),
            vmem((pw * kv_heads, pair), f32),
            vmem((pw * kv_heads, pair), bf16),
            vmem((chips, pw * kv_heads, pair), bf16),
            dma, dma, dma((chips,)), dma((chips,)), dma((chips,)), dma((chips,)), dma, dma,
        ]
    else:
        kvg_shape = (tok, kvc)
    context, input_grad, other = pl.pallas_call(
        functools.partial(fused_kernel, n, m, sum_seq),
        out_shape=[
            jax.ShapeDtypeStruct((tok, qc), bf16),
            jax.ShapeDtypeStruct((tok, ch), bf16),
            jax.ShapeDtypeStruct(kvg_shape, bf16),
        ],
        in_specs=[ANY] * 5 + [VMEM, SMEM],
        out_specs=[ANY, VMEM, ANY],
        scratch_shapes=scratch,
        compiler_params=pltpu.CompilerParams(
            vmem_limit_bytes=56 * 2**20, collective_id=0, has_side_effects=True
        ),
        name="fused",
    )(normed, out_cotangent, query_weight, wkv, out_weight, segments.reshape(-1, BLOCK), band_mask)
    if sum_seq:
        context, input_grad, kv_grad = written(context, input_grad, other)
    else:
        kv_grad = lax.dot_general(normed, other, (((0,), (0,)), ((), ())), preferred_element_type=f32)
        kv_grad = lax.psum(kv_grad, "seq")
    return context, input_grad, kv_grad.reshape(width, kv_heads, pair)


def solution(mesh):
    placed = (
        P("seq", None),
        P("seq", None),
        P(),
        P("seq", None),
        P(None, "mp"),
        P(None, "mp", None),
        P("mp", None),
    )
    return jax.shard_map(
        functools.partial(local, mesh.shape["seq"], mesh.shape["mp"]),
        mesh=mesh,
        in_specs=placed,
        out_specs=(P("seq", "mp"), P("seq", "mp"), P(None, "mp", None)),
        check_vma=False,
    )
```

profile of v0, /device:TPU:0, one launch (start us, length us, event | category | flops | bytes accessed | tf_op | source)
XLA Modules:
  0.0 71.4 jit_solution(13831513006791738378)
XLA Ops:
  0.6 68.0 %fused.1 = (bf16[512,512]{1,0:T(8,128)(2,1)}, bf16[512,512]{1,0:T(8,128)(2,1)}, bf16[4096,128]{1,0:T(8,128)(2,1)}) custom-call(bf16[512,2048]{1,0:T(8,128)(2,1)} %x_hbm.1, bf16[512,2048]{1,0:T(8,128)(2,1)} %oc_hbm.1, bf16[2048,512]{1,0:T(8,128)(2,1)} %wq_hbm.1, bf16[4096,128]{1,0:T(8,128)(2,1)} %bitcast.3, bf16[512,2048]{1,0:T(8,128)(2,1)} %wo_hbm.1, ...), custom_call_target="tpu_custom_call" | custom-call | tf_op jit(solution)/shard_map/fused/pallas_call | solution.py:531
  68.7 2.7 %write.1 = (bf16[512,512]{1,0:T(8,128)(2,1)}, bf16[512,512]{1,0:T(8,128)(2,1)}, f32[4096,128]{1,0:T(8,128)}) custom-call(bf16[512,512]{1,0:T(8,128)(2,1)} %get-tuple-element.9.ctx_hbm, bf16[512,512]{1,0:T(8,128)(2,1)} %get-tuple-element.10.ig_hbm, bf16[4096,128]{1,0:T(8,128)(2,1)} %get-tuple-element.11.kvg_hbm), custom_call_target="tpu_custom_call" | custom-call | tf_op jit(solution)/shard_map/write/pallas_call | solution.py:451
where the time goes:
time: 71.7 us; the launch traced here: 71.4 us
  Pallas kernels  70.8 us (99%)
    pallas_call x1, Pallas kernels, local(): pl.pallas_call(functools.partial(fused_kernel, n, m, sum_seq), out_shape=...  68 us
    pallas_call x1, Pallas kernels, written(): pl.pallas_call(write_kernel, out_shape=[jax.ShapeDtypeStruct(a.shape, t)...  2.75 us

commit v1 on v0

--- a/solution.py
+++ b/solution.py
@@ -15,6 +15,7 @@
 MARGIN = 2 * BLOCK
 WINDOW = BLOCK + 2 * MARGIN
 SCALE = 0.125
+AHEAD = 2
 
 MESH = pl.DeviceIdType.MESH
 NT = (((1,), (1,)), ((), ()))
@@ -423,6 +424,588 @@
         pl.when(has_right)(to_right.wait_send)
 
 
+def relay_kernel(n, ag, x_hbm, oc_hbm, wq_hbm, wkv_hbm, wo_hbm, seg_ref, band_ref,
+                 ctx_hbm, ig_ref, kvg_hbm, ctx_ref, raw, wide_raw, x_ref, oc_ref, wall, wo_ref, q_ref, dc_ref,
+                 kvx, kdocs, bias, grad, halo, hin, dall, wx, dout, dx, snd, rcv, tout, rin,
+                 gt, gsum, sib, quart, got, mine, mix, piece, sib2,
+                 ls, os, ks, kr, hs, hr, ss, sr, qs, qr, gs, gr, fs, fr,
+                 zhs, zhr, zas, zar, pls, plr, pfs, pfr, pss, psr,
+                 oqs, oqr, oks, okr, xqs, xqr, xks, xkr, rss, rsr, tos, tor):
+    tok, qc = q_ref.shape
+    kvc = kvx.shape[1]
+    ch = wall.shape[0] // 4
+    blocks = tok // BLOCK
+    kv_heads = kvc // (2 * HEAD_DIM)
+    wide = GROUP * HEAD_DIM
+    pair = 2 * HEAD_DIM
+    held = ag * BLOCK
+    me = lax.axis_index("seq")
+    z = lax.axis_index("mp")
+    core = me % 2
+    sibling = me + 1 - 2 * core
+    chip = me // 2
+    chips = n // 2
+    pr = ch // n
+    outer = (z == 0) | (z == 3)
+    inner = jnp.logical_not(outer)
+    partner = jnp.where(outer, jnp.where(z == 0, 1, 2), jnp.where(z == 1, 0, 3))
+    facing = 3 - z
+    facing_partner = 3 - partner
+
+    loads = [
+        pltpu.make_async_copy(src, dst, ls.at[i])
+        for i, (src, dst) in enumerate((
+            (wkv_hbm, raw),
+            (x_hbm, x_ref),
+            (wq_hbm, wall.at[:, pl.ds(0, qc)]),
+            (oc_hbm, oc_ref),
+            (wo_hbm, wo_ref),
+        ))
+    ]
+    for cp in loads:
+        cp.start()
+
+    def seq_dev(i):
+        return (i, z)
+
+    def mp_dev(i):
+        return (me, i)
+
+    barrier = pltpu.get_barrier_semaphore()
+    has_left, has_right = me > 0, me < n - 1
+    has_down, has_up = z > 0, z < 3
+
+    def greet(dev):
+        pl.semaphore_signal(barrier, inc=1, device_id=dev, device_id_type=MESH)
+
+    for there, dev in (
+        (has_left, seq_dev(me - 1)),
+        (has_right, seq_dev(me + 1)),
+        (has_down, mp_dev(z - 1)),
+        (has_up, mp_dev(z + 1)),
+    ):
+        @pl.when(there)
+        def _():
+            greet(dev)
+    for k in range(1, chips):
+        greet(seq_dev(((chip + k) % chips) * 2 + core))
+    peers = chips - 1
+    for there in (has_left, has_right, has_down, has_up):
+        peers = peers + there.astype(jnp.int32)
+    pl.semaphore_wait(barrier, peers)
+
+    def remote(src, dst, send, recv, dev):
+        return pltpu.make_async_remote_copy(
+            src_ref=src, dst_ref=dst, send_sem=send, recv_sem=recv, device_id=dev,
+            device_id_type=MESH)
+
+    qcols, kvcols = pl.ds(0, qc), pl.ds(qc, kvc)
+
+    def rows_of(c):
+        return pl.ds(pl.multiple_of(c * ch + me * pr, pr), pr)
+
+    sent_chunks = (partner, facing_partner, facing)
+    zh = [[], []]
+    for j, c in enumerate(sent_chunks):
+        zh[0].append(remote(wq_hbm.at[rows_of(c), :], wx.at[j, chip, core, :, qcols], zhs.at[0, j], zhr.at[0, j], mp_dev(partner)))
+        zh[1].append(remote(wall.at[rows_of(c), kvcols], wx.at[j, chip, core, :, kvcols], zhs.at[1, j], zhr.at[1, j], mp_dev(partner)))
+    za = [[], [], []]
+    if ag:
+        for j, c in enumerate((facing, facing_partner)):
+            za[0].append(remote(wq_hbm.at[rows_of(c), :], wx.at[3 + j, chip, core, :, qcols], zas.at[0, j], zar.at[0, j], mp_dev(facing)))
+            za[1].append(remote(wall.at[rows_of(c), kvcols], wx.at[3 + j, chip, core, :, kvcols], zas.at[1, j], zar.at[1, j], mp_dev(facing)))
+            za[2].append(remote(wx.at[1 + j, chip, core], wx.at[5 + j, chip, core], zas.at[2, j], zar.at[2, j], mp_dev(facing)))
+
+    def each(cps, what):
+        for cp in cps:
+            getattr(cp, what)()
+
+    @pl.when(outer)
+    def _():
+        each(zh[0], "start")
+
+    @pl.when(inner)
+    def _():
+        each(za[0], "start")
+
+    xchip, ychip = chip + 1 - 2 * (chip % 2), (chip + 2) % chips
+    dchip = (xchip + 2) % chips
+    sets = ((0, 3), (3, 2), (5, 2)) if ag else ((0, 3),)
+    half = pr // 2
+    to_x, to_y, via_x, via_y, to_sib = [], [], [], [], []
+    for i, (first, count) in enumerate(sets):
+        ksl = pl.ds(first, count)
+        own = wx.at[ksl, chip, core]
+        to_x.append(remote(own, own, pls.at[0, i], plr.at[0, i], seq_dev(xchip * 2 + core)))
+        to_y.append(remote(own, own, pls.at[1, i], plr.at[1, i], seq_dev(ychip * 2 + core)))
+        lo = wx.at[ksl, xchip, core, pl.ds(0, half)]
+        hi = wx.at[ksl, ychip, core, pl.ds(half, half)]
+        via_y.append(remote(lo, lo, pfs.at[0, i], pfr.at[0, i], seq_dev(ychip * 2 + core)))
+        via_x.append(remote(hi, hi, pfs.at[1, i], pfr.at[1, i], seq_dev(xchip * 2 + core)))
+        row = []
+        for j, c in enumerate((chip, xchip, ychip, dchip)):
+            part = wx.at[ksl, c, core]
+            row.append(remote(part, part, pss.at[i, j], psr.at[i, j], seq_dev(sibling)))
+        to_sib.append(row)
+
+    def plane_start(i):
+        to_x[i].start()
+        to_y[i].start()
+        to_sib[i][0].start()
+
+    def plane_wait_x(i):
+        first, count = sets[i]
+        dst = wx.at[pl.ds(first, count), xchip, core]
+        remote(dst, dst, pls.at[0, i], plr.at[0, i], seq_dev(sibling)).wait_recv()
+
+    def plane_wait_y(i):
+        first, count = sets[i]
+        dst = wx.at[pl.ds(first, count), ychip, core]
+        remote(dst, dst, pls.at[1, i], plr.at[1, i], seq_dev(sibling)).wait_recv()
+
+    def plane_relay(i):
+        plane_wait_x(i)
+        via_y[i].start()
+        to_sib[i][1].start()
+        plane_wait_y(i)
+        via_x[i].start()
+        to_sib[i][2].start()
+
+    def plane_pair(i):
+        first, count = sets[i]
+        for f, s in enumerate((pl.ds(0, half), pl.ds(half, half))):
+            dst = wx.at[pl.ds(first, count), dchip, core, s]
+            remote(dst, dst, pfs.at[f, i], pfr.at[f, i], seq_dev(sibling)).wait_recv()
+        to_sib[i][3].start()
+
+    def plane_done(i):
+        first, count = sets[i]
+        for j, c in enumerate((chip, xchip, ychip, dchip)):
+            dst = wx.at[pl.ds(first, count), c, 1 - core]
+            remote(dst, dst, pss.at[i, j], psr.at[i, j], seq_dev(sibling)).wait_recv()
+
+    loads[0].wait()
+    span = wide_raw.shape[0] // kv_heads
+
+    @pl.loop(0, wall.shape[0] // span)
+    def _(i):
+        wide_raw[...] = raw[pl.ds(pl.multiple_of(i * span * kv_heads, 256), span * kv_heads), :].astype(f32)
+        for g in range(kv_heads):
+            wall[pl.ds(pl.multiple_of(i * span, 256), span), qc + g * 128 : qc + (g + 1) * 128] = (
+                wide_raw[pl.ds(g, span, stride=kv_heads), :].astype(bf16)
+            )
+
+    loads[1].wait()
+
+    @pl.loop(0, tok // 256)
+    def _(i):
+        r = pl.ds(pl.multiple_of(i * 256, 256), 256)
+        ro = pl.ds(pl.multiple_of(i * 256 + MARGIN, 256), 256)
+        kvx[ro, :] = jnp.dot(x_ref[r, :], wall[:, qc:], preferred_element_type=f32).astype(bf16)
+
+    before, after = pl.ds(0, MARGIN), pl.ds(MARGIN + tok, MARGIN)
+    kv_left = remote(kvx.at[pl.ds(MARGIN, MARGIN)], kvx.at[after], ks.at[0], kr.at[0], seq_dev(me - 1))
+    kv_right = remote(kvx.at[pl.ds(tok, MARGIN)], kvx.at[before], ks.at[1], kr.at[1], seq_dev(me + 1))
+    pl.when(has_left)(kv_left.start)
+    pl.when(has_right)(kv_right.start)
+
+    @pl.when(outer)
+    def _():
+        each(zh[1], "start")
+
+    @pl.when(inner)
+    def _():
+        each(za[1], "start")
+
+    for kb in range(blocks + 4):
+        row = me * blocks + kb - 2
+        inside = (row >= 0) & (row < n * blocks)
+        docs = seg_ref[pl.ds(jnp.clip(row, 0, n * blocks - 1), 1), :]
+        docs = jnp.where(inside, docs, -1)
+        kdocs[kb] = jnp.transpose(jnp.broadcast_to(docs, (BLOCK, BLOCK)))
+
+    @pl.loop(0, blocks)
+    def _(b):
+        qdoc = seg_ref[pl.ds(me * blocks + b, 1), :]
+        for o in range(5):
+            same = kdocs[b + o] == qdoc
+            if o != 2:
+                same = same & (band_ref[b, o if o < 2 else o - 1] == 1)
+            bias[b, o * BLOCK : (o + 1) * BLOCK, :] = jnp.where(same, 0.0, -1e30).astype(f32)
+
+    grad[...] = jnp.zeros_like(grad)
+    loads[2].wait()
+
+    @pl.loop(0, tok // 256)
+    def _(i):
+        r = pl.ds(pl.multiple_of(i * 256, 256), 256)
+        q_ref[r, :] = jnp.dot(x_ref[r, :], wall[:, :qc], preferred_element_type=f32).astype(bf16)
+
+    loads[3].wait()
+    loads[4].wait()
+
+    @pl.loop(0, tok // 256)
+    def _(i):
+        r = pl.ds(pl.multiple_of(i * 256, 256), 256)
+        dc_ref[r, :] = lax.dot_general(
+            oc_ref[r, :], wo_ref[...], NT, preferred_element_type=f32
+        ).astype(bf16)
+
+    @pl.when(jnp.logical_not(has_left))
+    def _():
+        kvx[before, :] = jnp.zeros((MARGIN, kvc), bf16)
+        for g in range(kv_heads):
+            hin[1, g] = jnp.zeros(hin.shape[2:], bf16)
+
+    @pl.when(jnp.logical_not(has_right))
+    def _():
+        kvx[after, :] = jnp.zeros((MARGIN, kvc), bf16)
+        for g in range(kv_heads):
+            hin[0, g] = jnp.zeros(hin.shape[2:], bf16)
+
+    @pl.when(inner)
+    def _():
+        each(zh[0], "wait_recv")
+        each(zh[1], "wait_recv")
+        plane_start(0)
+        each(za[2], "start")
+        each(za[0], "wait_recv")
+        each(za[1], "wait_recv")
+        plane_start(1)
+
+    pl.when(has_left)(kv_right.wait_recv)
+    pl.when(has_right)(kv_left.wait_recv)
+
+    def block_rows(b):
+        return pl.ds(pl.multiple_of(b * BLOCK, BLOCK), BLOCK)
+
+    def dq_out(g, b):
+        at = (block_rows(b), pl.ds(g * wide, wide))
+        return remote(dall.at[at], dout.at[at], oqs.at[g, b], oqr.at[g, b], mp_dev(partner))
+
+    def dq_across(which, g, b):
+        at = (block_rows(b), pl.ds(g * wide, wide))
+        src = dall.at[at] if which == 0 else dout.at[at]
+        return remote(src, dx.at[(which,) + at], xqs.at[which, g, b], xqr.at[which, g, b], mp_dev(facing))
+
+    def dkv_cols(g):
+        return pl.ds(qc + g * pair, pair)
+
+    def dkv_out(g, early):
+        rows = pl.ds(0, held) if early else pl.ds(held, tok - held)
+        at = (rows, dkv_cols(g))
+        i = 1 if early else 0
+        return remote(dall.at[at], dout.at[at], oks.at[g, i], okr.at[g, i], mp_dev(partner))
+
+    def dkv_across(which, g):
+        at = (pl.ds(0, held), dkv_cols(g))
+        src = dall.at[at] if which == 0 else dout.at[at]
+        return remote(src, dx.at[(which,) + at], xks.at[which, g], xkr.at[which, g], mp_dev(facing))
+
+    def halo_left(g):
+        return remote(halo.at[0, g], hin.at[0, g], hs.at[0, g], hr.at[0, g], seq_dev(me - 1))
+
+    def halo_right(g):
+        return remote(halo.at[1, g], hin.at[1, g], hs.at[1, g], hr.at[1, g], seq_dev(me + 1))
+
+    def finish_late(g):
+        pl.when(has_right)(halo_left(g).wait_recv)
+        dall[held:, qc + g * pair : qc + (g + 1) * pair] = (
+            grad[MARGIN + held : MARGIN + tok, g * pair : (g + 1) * pair] + hin[0, g].astype(f32)
+        ).astype(bf16)
+        pl.when(outer)(dkv_out(g, False).start)
+
+    def finish_early(g):
+        pl.when(has_left)(halo_right(g).wait_recv)
+        dall[:held, qc + g * pair : qc + (g + 1) * pair] = (
+            grad[MARGIN : MARGIN + held, g * pair : (g + 1) * pair] + hin[1, g].astype(f32)
+        ).astype(bf16)
+        pl.when(outer)(dkv_out(g, True).start)
+        pl.when(inner)(dkv_across(0, g).start)
+
+    for g in range(kv_heads):
+        cols = slice(g * wide, (g + 1) * wide)
+        kcols = slice(g * pair, (g + 1) * pair)
+
+        @pl.loop(0, blocks)
+        def _(b):
+            first = pl.multiple_of(b * BLOCK, BLOCK)
+            qt = side_by_side(jnp.transpose(q_ref[pl.ds(first, BLOCK), cols] * SCALE))
+            dct = side_by_side(jnp.transpose(dc_ref[pl.ds(first, BLOCK), cols]))
+            zero = jnp.zeros_like(qt)
+            qz = jnp.concatenate([qt, zero], axis=0)
+            dcz = jnp.concatenate([zero, dct], axis=0)
+            kv = kvx[pl.ds(first, WINDOW), kcols]
+            kvt = jnp.transpose(kv)
+            s = jnp.dot(kv, qz, preferred_element_type=f32)
+            s = s + jnp.concatenate([bias[b]] * GROUP, axis=1)
+            p = jnp.exp(s - jnp.max(s, axis=0, keepdims=True))
+            w = p * (1.0 / jnp.sum(p, axis=0, keepdims=True))
+            wh = w.astype(bf16)
+            ctx = jnp.dot(kvt[HEAD_DIM:], wh, preferred_element_type=f32).astype(bf16)
+            delta = jnp.sum(dct.astype(f32) * ctx.astype(f32), axis=0, keepdims=True)
+            dp = jnp.dot(kv, dcz, preferred_element_type=f32)
+            ds = (w * (dp - delta)).astype(bf16)
+            dq = jnp.dot(kvt[:HEAD_DIM], ds, preferred_element_type=f32) * SCALE
+            ctx_ref[pl.ds(first, BLOCK), cols] = jnp.transpose(stacked(ctx))
+            dall[pl.ds(first, BLOCK), cols] = jnp.transpose(stacked(dq.astype(bf16)))
+            d_kv = lax.dot_general(ds, qz, NT, preferred_element_type=f32)
+            d_kv = d_kv + lax.dot_general(wh, dcz, NT, preferred_element_type=f32)
+            grad[pl.ds(first, WINDOW), kcols] += d_kv
+
+            @pl.when(outer)
+            def _():
+                dq_out(g, b).start()
+
+            @pl.when(inner & (b < ag))
+            def _():
+                dq_across(0, g, b).start()
+
+            @pl.when(inner & (b >= 2) & (b < ag + 2))
+            def _():
+                dq_out(g, b - 2).wait_recv()
+                dq_across(1, g, b - 2).start()
+
+            @pl.when(b == 1)
+            def _():
+                halo[0, g] = grad[:MARGIN, kcols].astype(bf16)
+                pl.when(has_left)(halo_left(g).start)
+
+            if g == 1:
+                @pl.when(inner & (b == 0))
+                def _():
+                    plane_relay(0)
+                    each(za[2], "wait_recv")
+                    plane_start(2)
+
+                @pl.when(b == 1)
+                def _():
+                    finish_early(0)
+                    finish_late(0)
+
+                @pl.when(inner & (b == blocks - 1))
+                def _():
+                    plane_relay(1)
+
+        halo[1, g] = grad[MARGIN + tok :, kcols].astype(bf16)
+        pl.when(has_right)(halo_right(g).start)
+
+    leave = [pltpu.make_async_copy(ctx_ref, ctx_hbm, os.at[0])]
+    leave[0].start()
+    finish_late(1)
+
+    @pl.when(inner)
+    def _():
+        dkv_out(0, True).wait_recv()
+        dkv_across(1, 0).start()
+
+    finish_early(1)
+    pl.when(inner)(functools.partial(plane_pair, 0))
+
+    pw = gt.shape[3]
+    gr_rows = pw * kv_heads
+    dkvt = jnp.transpose(dall[:, qc:])
+    for k in range(2):
+        part = (1 - core) if k == 0 else core
+
+        @pl.loop(0, chips)
+        def _(j):
+            cols = pl.ds(pl.multiple_of((2 * j + part) * pw, pw), pw)
+            prod = jnp.dot(dkvt, x_ref[:, cols], preferred_element_type=f32)
+            if k == 0:
+                gt[0, j] = prod.astype(bf16)
+            else:
+                gsum[j] = prod
+
+        if k == 0:
+            swap = remote(gt.at[0], sib, ss, sr, seq_dev(sibling))
+            swap.start()
+
+    def chunk(c):
+        return pl.ds(pl.multiple_of(c * ch, ch), ch)
+
+    def times_own(r, c):
+        return lax.dot_general(dall[r, :], wall[chunk(c), :], NT, preferred_element_type=f32)
+
+    def times_sent(d, k):
+        return lax.dot_general(d, wx[k].reshape(ch, qc + kvc), NT, preferred_element_type=f32)
+
+    tile = 256 if ag % 2 == 0 else 128
+    summed = tok - held
+
+    def sum_piece(slot, i):
+        at = (slot, pl.ds(i * BLOCK, BLOCK))
+        return remote(snd.at[at], rcv.at[at], rss.at[slot, i], rsr.at[slot, i], mp_dev(facing))
+
+    def out_piece(i):
+        at = block_rows(i)
+        return remote(tout.at[at], rin.at[at], tos.at[i], tor.at[i], mp_dev(partner))
+
+    steps = tile // BLOCK
+
+    @pl.when(inner)
+    def _():
+        for g in range(kv_heads):
+            for b in range(ag, blocks):
+                dq_out(g, b).wait_recv()
+            dkv_out(g, False).wait_recv()
+        plane_done(0)
+        for slot in (1, 0):
+            c = facing_partner if slot == 1 else facing
+            for t in range(summed // tile):
+                r = slice(held + t * tile, held + (t + 1) * tile)
+                snd[slot, t * tile : (t + 1) * tile, :] = (
+                    times_own(r, c) + times_sent(dout[r, :], slot + 1)
+                ).astype(bf16)
+                for i in range(t * steps, (t + 1) * steps):
+                    sum_piece(slot, i).start()
+            if slot == 1:
+                dkv_out(1, True).wait_recv()
+                dkv_across(1, 1).start()
+                plane_relay(2)
+                plane_pair(1)
+
+    swap.wait_recv()
+
+    def other(k):
+        return (chip + k) % chips
+
+    sends = []
+    for k in range(1, chips):
+        j = other(k)
+        gt[1, j] = (gsum[j] + sib[j].astype(f32)).astype(bf16)
+        cp = remote(gt.at[1, j], quart.at[k], qs.at[k], qr.at[k], seq_dev(j * 2 + core))
+        cp.start()
+        sends.append(cp)
+    mine[...] = gsum[chip] + sib[chip].astype(f32)
+    swap.wait_send()
+
+    @pl.when(inner)
+    def _():
+        for i in range(summed // BLOCK):
+            r = slice(held + i * BLOCK, held + (i + 1) * BLOCK)
+            own = times_own(r, partner)
+            sum_piece(1, i).wait_recv()
+            tout[r, :] = (own + rcv[1, i * BLOCK : (i + 1) * BLOCK, :].astype(f32)).astype(bf16)
+            out_piece(ag + i).start()
+
+    for cp in sends:
+        cp.wait_recv()
+    for k in range(1, chips):
+        mine[...] += quart[k].astype(f32)
+    for cp in sends:
+        cp.wait_send()
+    done = jnp.transpose(mine[...])
+    for g in range(kv_heads):
+        kcols = slice(g * pair, (g + 1) * pair)
+        mix[pl.ds(g, pw, stride=kv_heads), :] = done[:, kcols]
+    piece[...] = mix[...].astype(bf16)
+    sends = []
+    for k in range(1, chips):
+        cp = remote(piece, got.at[k], gs.at[k], gr.at[k], seq_dev(other(k) * 2 + core))
+        cp.start()
+        sends.append(cp)
+
+    if ag:
+        @pl.when(inner)
+        def _():
+            for which in range(2):
+                for g in range(kv_heads):
+                    for b in range(ag):
+                        dq_across(which, g, b).wait_recv()
+                    dkv_across(which, g).wait_recv()
+            plane_pair(2)
+            plane_done(1)
+            plane_done(2)
+            for t in range(held // tile):
+                r = slice(t * tile, (t + 1) * tile)
+                tout[r, :] = (
+                    times_own(r, partner) + times_sent(dx[0, r, :], 4) + times_sent(dx[1, r, :], 6)
+                ).astype(bf16)
+                for i in range(t * steps, (t + 1) * steps):
+                    out_piece(i).start()
+            for t in range(held // tile):
+                r = slice(t * tile, (t + 1) * tile)
+                ig_ref[r, :] = (
+                    times_own(r, z) + times_sent(dout[r, :], 0)
+                    + times_sent(dx[0, r, :], 3) + times_sent(dx[1, r, :], 5)
+                ).astype(bf16)
+
+    got[0] = piece[...]
+    for cp in sends:
+        cp.wait()
+    swap = remote(got, sib2, fs, fr, seq_dev(sibling))
+    swap.start()
+    for k in range(chips):
+        src = (chip + chips - k) % chips
+        rows = pl.ds(pl.multiple_of((2 * src + core) * gr_rows, gr_rows), gr_rows)
+        leave.append(pltpu.make_async_copy(got.at[k], kvg_hbm.at[rows], os.at[1 + k]))
+        leave[-1].start()
+    swap.wait_recv()
+    for k in range(chips):
+        src = (chip + chips - k) % chips
+        rows = pl.ds(pl.multiple_of((2 * src + 1 - core) * gr_rows, gr_rows), gr_rows)
+        leave.append(pltpu.make_async_copy(sib2.at[k], kvg_hbm.at[rows], os.at[1 + chips + k]))
+        leave[-1].start()
+    swap.wait_send()
+
+    @pl.when(inner)
+    def _():
+        for t in range(summed // tile):
+            for i in range(t * steps, (t + 1) * steps):
+                sum_piece(0, i).wait_recv()
+            r = slice(held + t * tile, held + (t + 1) * tile)
+            ig_ref[r, :] = (
+                times_own(r, z) + times_sent(dout[r, :], 0)
+                + rcv[0, t * tile : (t + 1) * tile, :].astype(f32)
+            ).astype(bf16)
+
+    @pl.when(outer)
+    def _():
+        order = list(range(ag, blocks)) + list(range(ag))
+        for i in order:
+            r = slice(i * BLOCK, (i + 1) * BLOCK)
+            own = times_own(r, z)
+            out_piece(i).wait_recv()
+            ig_ref[r, :] = (own + rin[r, :].astype(f32)).astype(bf16)
+
+    @pl.when(outer)
+    def _():
+        for g in range(kv_heads):
+            for b in range(blocks):
+                dq_out(g, b).wait_send()
+            dkv_out(g, False).wait_send()
+            if ag:
+                dkv_out(g, True).wait_send()
+        each(zh[0], "wait_send")
+        each(zh[1], "wait_send")
+
+    @pl.when(inner)
+    def _():
+        for which in range(2 if ag else 0):
+            for g in range(kv_heads):
+                for b in range(ag):
+                    dq_across(which, g, b).wait_send()
+                dkv_across(which, g).wait_send()
+        for slot in range(2):
+            for i in range(blocks - ag):
+                sum_piece(slot, i).wait_send()
+        for i in range(blocks):
+            out_piece(i).wait_send()
+        for group in za:
+            each(group, "wait_send")
+        for group in (to_x, to_y, via_x, via_y, *to_sib):
+            each(group, "wait_send")
+
+    for cp in leave:
+        cp.wait()
+    pl.when(has_left)(kv_left.wait_send)
+    pl.when(has_right)(kv_right.wait_send)
+    for g in range(kv_heads):
+        pl.when(has_left)(halo_left(g).wait_send)
+        pl.when(has_right)(halo_right(g).wait_send)
+
+
 def write_kernel(ctx_hbm, ig_hbm, kvg_hbm, ctx_out, ig_out, kvg_out, half, full, ctx_mid, ig_mid, ins, outs):
     pieces, rows = half.shape[0], half.shape[1]
     loads, stores = [], []
@@ -482,6 +1065,7 @@
     chips = n // 2
     dma = pltpu.SemaphoreType.DMA
     vmem = pltpu.VMEM
+    relay = n == 8 and m == 4 and kv_heads == 2 and tok == 4 * BLOCK and sum_seq
     scratch = [
         vmem((tok, qc), bf16),
         vmem((width * kv_heads, pair), bf16),
@@ -514,22 +1098,82 @@
     ]
     if sum_seq:
         kvg_shape = (width * kv_heads, pair)
-        scratch += [
-            vmem((2, chips, kvc, pw), bf16),
-            vmem((chips, kvc, pw), f32),
-            vmem((chips, kvc, pw), bf16),
-            vmem((chips, kvc, pw), bf16),
-            vmem((chips, pw * kv_heads, pair), bf16),
-            vmem((kvc, pw), f32),
-            vmem((pw * kv_heads, pair), f32),
-            vmem((pw * kv_heads, pair), bf16),
-            vmem((chips, pw * kv_heads, pair), bf16),
-            dma, dma, dma((chips,)), dma((chips,)), dma((chips,)), dma((chips,)), dma, dma,
-        ]
+        if not relay:
+            scratch += [
+                vmem((2, chips, kvc, pw), bf16),
+                vmem((chips, kvc, pw), f32),
+                vmem((chips, kvc, pw), bf16),
+                vmem((chips, kvc, pw), bf16),
+                vmem((chips, pw * kv_heads, pair), bf16),
+                vmem((kvc, pw), f32),
+                vmem((pw * kv_heads, pair), f32),
+                vmem((pw * kv_heads, pair), bf16),
+                vmem((chips, pw * kv_heads, pair), bf16),
+                dma, dma, dma((chips,)), dma((chips,)), dma((chips,)), dma((chips,)), dma, dma,
+            ]
     else:
         kvg_shape = (tok, kvc)
+    ag = AHEAD
+    held = ag * BLOCK
+    relay_scratch = [
+        vmem((tok, qc), bf16),
+        vmem((width * kv_heads, pair), bf16),
+        vmem((256 * kv_heads, pair), f32),
+        vmem((tok, width), bf16),
+        vmem((tok, width), bf16),
+        vmem((width, qc + kvc), bf16),
+        vmem((qc, width), bf16),
+        vmem((tok, qc), bf16),
+        vmem((tok, qc), bf16),
+        vmem((tok + 2 * MARGIN, kvc), bf16),
+        vmem((blocks + 4, BLOCK, BLOCK), jnp.int32),
+        vmem((blocks, WINDOW, BLOCK), f32),
+        vmem((tok + 2 * MARGIN, kvc), f32),
+        vmem((2, kv_heads, MARGIN, pair), bf16),
+        vmem((2, kv_heads, MARGIN, pair), bf16),
+        vmem((tok, qc + kvc), bf16),
+        vmem((7 if ag else 3, max(chips, 1), 2, max(ch // n, 8), qc + kvc), bf16),
+        vmem((tok, qc + kvc), bf16),
+        vmem((2, max(held, BLOCK), qc + kvc), bf16),
+        vmem((2, max(tok - held, BLOCK), ch), bf16),
+        vmem((2, max(tok - held, BLOCK), ch), bf16),
+        vmem((tok, ch), bf16),
+        vmem((tok, ch), bf16),
+        vmem((2, chips, kvc, pw), bf16),
+        vmem((chips, kvc, pw), f32),
+        vmem((chips, kvc, pw), bf16),
+        vmem((chips, kvc, pw), bf16),
+        vmem((chips, pw * kv_heads, pair), bf16),
+        vmem((kvc, pw), f32),
+        vmem((pw * kv_heads, pair), f32),
+        vmem((pw * kv_heads, pair), bf16),
+        vmem((chips, pw * kv_heads, pair), bf16),
+        dma((5,)),
+        dma((1 + n,)),
+        dma((2,)),
+        dma((2,)),
+        dma((2, kv_heads)),
+        dma((2, kv_heads)),
+        dma, dma, dma((chips,)), dma((chips,)), dma((chips,)), dma((chips,)), dma, dma,
+        dma((2, 3)), dma((2, 3)),
+        dma((3, 2)), dma((3, 2)),
+        dma((2, 3)), dma((2, 3)),
+        dma((2, 3)), dma((2, 3)),
+        dma((3, 4)), dma((3, 4)),
+        dma((kv_heads, blocks)), dma((kv_heads, blocks)),
+        dma((kv_heads, 2)), dma((kv_heads, 2)),
+        dma((2, kv_heads, blocks)), dma((2, kv_heads, blocks)),
+        dma((2, kv_heads)), dma((2, kv_heads)),
+        dma((2, blocks)), dma((2, blocks)),
+        dma((blocks,)), dma((blocks,)),
+    ]
+    if relay:
+        scratch = relay_scratch
+        body = functools.partial(relay_kernel, n, ag)
+    else:
+        body = functools.partial(fused_kernel, n, m, sum_seq)
     context, input_grad, other = pl.pallas_call(
-        functools.partial(fused_kernel, n, m, sum_seq),
+        body,
         out_shape=[
             jax.ShapeDtypeStruct((tok, qc), bf16),
             jax.ShapeDtypeStruct((tok, ch), bf16),

time: 71.7 us -> 65.3 us (0.911)
  Pallas kernels: 70.8 us -> 64.4 us
    pallas_call x1, Pallas kernels: 68 us -> 61.7 us  [local(): pl.pallas_call(body, out_shape=[jax.ShapeDtypeStruct((tok, qc), bf16), ja...]
where the time goes in v1:
time: 65.3 us; the launch traced here: 65.1 us
  Pallas kernels  64.4 us (99%)
    pallas_call x1, Pallas kernels, local(): pl.pallas_call(body, out_shape=[jax.ShapeDtypeStruct((tok, qc), bf16), ja...  61.7 us
    pallas_call x1, Pallas kernels, written(): pl.pallas_call(write_kernel, out_shape=[jax.ShapeDtypeStruct(a.shape, t)...  2.75 us

profile of v1, /device:TPU:0, one launch (start us, length us, event | category | flops | bytes accessed | tf_op | source)
XLA Modules:
  0.0 65.1 jit_solution(8489187548316629326)
XLA Ops:
  0.6 61.7 %fused.1 = (bf16[512,512]{1,0:T(8,128)(2,1)}, bf16[512,512]{1,0:T(8,128)(2,1)}, bf16[4096,128]{1,0:T(8,128)(2,1)}) custom-call(bf16[512,2048]{1,0:T(8,128)(2,1)} %x_hbm.1, bf16[512,2048]{1,0:T(8,128)(2,1)} %oc_hbm.1, bf16[2048,512]{1,0:T(8,128)(2,1)} %wq_hbm.1, bf16[4096,128]{1,0:T(8,128)(2,1)} %bitcast.3, bf16[512,2048]{1,0:T(8,128)(2,1)} %wo_hbm.1, ...), custom_call_target="tpu_custom_call" | custom-call | tf_op jit(solution)/shard_map/fused/pallas_call | solution.py:1175
  62.3 2.7 %write.1 = (bf16[512,512]{1,0:T(8,128)(2,1)}, bf16[512,512]{1,0:T(8,128)(2,1)}, f32[4096,128]{1,0:T(8,128)}) custom-call(bf16[512,512]{1,0:T(8,128)(2,1)} %get-tuple-element.9.ctx_hbm, bf16[512,512]{1,0:T(8,128)(2,1)} %get-tuple-element.10.ig_hbm, bf16[4096,128]{1,0:T(8,128)(2,1)} %get-tuple-element.11.kvg_hbm), custom_call_target="tpu_custom_call" | custom-call | tf_op jit(solution)/shard_map/write/pallas_call | solution.py:1034

commit v2 on v1

--- a/solution.py
+++ b/solution.py
@@ -426,11 +426,11 @@
 
 def relay_kernel(n, ag, x_hbm, oc_hbm, wq_hbm, wkv_hbm, wo_hbm, seg_ref, band_ref,
                  ctx_hbm, ig_ref, kvg_hbm, ctx_ref, raw, wide_raw, x_ref, oc_ref, wall, wo_ref, q_ref, dc_ref,
-                 kvx, kdocs, bias, grad, halo, hin, dall, wx, dout, dx, snd, rcv, tout, rin,
+                 kvx, kdocs, bias, grad, halo, hin, dall, wx, dout, dx, snd, rcv, tout, rin, part,
                  gt, gsum, sib, quart, got, mine, mix, piece, sib2,
                  ls, os, ks, kr, hs, hr, ss, sr, qs, qr, gs, gr, fs, fr,
                  zhs, zhr, zas, zar, pls, plr, pfs, pfr, pss, psr,
-                 oqs, oqr, oks, okr, xqs, xqr, xks, xkr, rss, rsr, tos, tor):
+                 oqs, oqr, oks, okr, xqs, xqr, xks, xkr, rss, rsr, tos, tor, fas, far):
     tok, qc = q_ref.shape
     kvc = kvx.shape[1]
     ch = wall.shape[0] // 4
@@ -504,17 +504,21 @@
     def rows_of(c):
         return pl.ds(pl.multiple_of(c * ch + me * pr, pr), pr)
 
-    sent_chunks = (partner, facing_partner, facing)
+    sent_chunks = (facing_partner, facing)
     zh = [[], []]
     for j, c in enumerate(sent_chunks):
         zh[0].append(remote(wq_hbm.at[rows_of(c), :], wx.at[j, chip, core, :, qcols], zhs.at[0, j], zhr.at[0, j], mp_dev(partner)))
         zh[1].append(remote(wall.at[rows_of(c), kvcols], wx.at[j, chip, core, :, kvcols], zhs.at[1, j], zhr.at[1, j], mp_dev(partner)))
     za = [[], [], []]
     if ag:
-        for j, c in enumerate((facing, facing_partner)):
-            za[0].append(remote(wq_hbm.at[rows_of(c), :], wx.at[3 + j, chip, core, :, qcols], zas.at[0, j], zar.at[0, j], mp_dev(facing)))
-            za[1].append(remote(wall.at[rows_of(c), kvcols], wx.at[3 + j, chip, core, :, kvcols], zas.at[1, j], zar.at[1, j], mp_dev(facing)))
-            za[2].append(remote(wx.at[1 + j, chip, core], wx.at[5 + j, chip, core], zas.at[2, j], zar.at[2, j], mp_dev(facing)))
+        za.append([])
+        for j, c in enumerate((facing_partner, facing)):
+            za[0].append(remote(wq_hbm.at[rows_of(c), :], wx.at[(2, 4)[j], chip, core, :, qcols], zas.at[0, j], zar.at[0, j], mp_dev(facing)))
+            za[1].append(remote(wall.at[rows_of(c), kvcols], wx.at[(2, 4)[j], chip, core, :, kvcols], zas.at[1, j], zar.at[1, j], mp_dev(facing)))
+            for i, cols in enumerate((qcols, kvcols)):
+                za[2 + i].append(remote(
+                    wx.at[1 - j, chip, core, :, cols], wx.at[(3, 5)[j], chip, core, :, cols],
+                    zas.at[2 + i, j], zar.at[2 + i, j], mp_dev(facing)))
 
     def each(cps, what):
         for cp in cps:
@@ -530,7 +534,7 @@
 
     xchip, ychip = chip + 1 - 2 * (chip % 2), (chip + 2) % chips
     dchip = (xchip + 2) % chips
-    sets = ((0, 3), (3, 2), (5, 2)) if ag else ((0, 3),)
+    sets = ((0, 2), (2, 2), (4, 2))
     half = pr // 2
     to_x, to_y, via_x, via_y, to_sib = [], [], [], [], []
     for i, (first, count) in enumerate(sets):
@@ -544,8 +548,8 @@
         via_x.append(remote(hi, hi, pfs.at[1, i], pfr.at[1, i], seq_dev(xchip * 2 + core)))
         row = []
         for j, c in enumerate((chip, xchip, ychip, dchip)):
-            part = wx.at[ksl, c, core]
-            row.append(remote(part, part, pss.at[i, j], psr.at[i, j], seq_dev(sibling)))
+            block = wx.at[ksl, c, core]
+            row.append(remote(block, block, pss.at[i, j], psr.at[i, j], seq_dev(sibling)))
         to_sib.append(row)
 
     def plane_start(i):
@@ -595,6 +599,14 @@
                 wide_raw[pl.ds(g, span, stride=kv_heads), :].astype(bf16)
             )
 
+    @pl.when(outer)
+    def _():
+        each(zh[1], "start")
+
+    @pl.when(inner)
+    def _():
+        each(za[1], "start")
+
     loads[1].wait()
 
     @pl.loop(0, tok // 256)
@@ -608,14 +620,6 @@
     kv_right = remote(kvx.at[pl.ds(tok, MARGIN)], kvx.at[before], ks.at[1], kr.at[1], seq_dev(me + 1))
     pl.when(has_left)(kv_left.start)
     pl.when(has_right)(kv_right.start)
-
-    @pl.when(outer)
-    def _():
-        each(zh[1], "start")
-
-    @pl.when(inner)
-    def _():
-        each(za[1], "start")
 
     for kb in range(blocks + 4):
         row = me * blocks + kb - 2
@@ -636,10 +640,21 @@
     grad[...] = jnp.zeros_like(grad)
     loads[2].wait()
 
+    @pl.when(inner)
+    def _():
+        each(zh[0], "wait_recv")
+        each(za[2], "start")
+
     @pl.loop(0, tok // 256)
     def _(i):
         r = pl.ds(pl.multiple_of(i * 256, 256), 256)
         q_ref[r, :] = jnp.dot(x_ref[r, :], wall[:, :qc], preferred_element_type=f32).astype(bf16)
+
+    @pl.when(inner)
+    def _():
+        each(zh[1], "wait_recv")
+        each(za[3], "start")
+        plane_start(0)
 
     loads[3].wait()
     loads[4].wait()
@@ -663,16 +678,6 @@
         for g in range(kv_heads):
             hin[0, g] = jnp.zeros(hin.shape[2:], bf16)
 
-    @pl.when(inner)
-    def _():
-        each(zh[0], "wait_recv")
-        each(zh[1], "wait_recv")
-        plane_start(0)
-        each(za[2], "start")
-        each(za[0], "wait_recv")
-        each(za[1], "wait_recv")
-        plane_start(1)
-
     pl.when(has_left)(kv_right.wait_recv)
     pl.when(has_right)(kv_left.wait_recv)
 
@@ -701,6 +706,10 @@
         at = (pl.ds(0, held), dkv_cols(g))
         src = dall.at[at] if which == 0 else dout.at[at]
         return remote(src, dx.at[(which,) + at], xks.at[which, g], xkr.at[which, g], mp_dev(facing))
+
+    def dkv_rest_across(g):
+        at = (pl.ds(held, tok - held), dkv_cols(g))
+        return remote(dout.at[at], dx.at[(1,) + at], xks.at[2, g], xkr.at[2, g], mp_dev(facing))
 
     def halo_left(g):
         return remote(halo.at[0, g], hin.at[0, g], hs.at[0, g], hr.at[0, g], seq_dev(me - 1))
@@ -771,12 +780,20 @@
                 halo[0, g] = grad[:MARGIN, kcols].astype(bf16)
                 pl.when(has_left)(halo_left(g).start)
 
-            if g == 1:
-                @pl.when(inner & (b == 0))
+            if g == 0:
+                @pl.when(inner & (b == 1))
+                def _():
+                    each(za[0] + za[1] + za[2] + za[3], "wait_recv")
+                    plane_start(1)
+
+                @pl.when(inner & (b == blocks - 1))
                 def _():
                     plane_relay(0)
-                    each(za[2], "wait_recv")
-                    plane_start(2)
+
+            if g == 1:
+                @pl.when(inner & (b == 1))
+                def _():
+                    plane_relay(1)
 
                 @pl.when(b == 1)
                 def _():
@@ -785,10 +802,33 @@
 
                 @pl.when(inner & (b == blocks - 1))
                 def _():
-                    plane_relay(1)
+                    plane_pair(0)
 
         halo[1, g] = grad[MARGIN + tok :, kcols].astype(bf16)
         pl.when(has_right)(halo_right(g).start)
+
+    def chunk(c):
+        return pl.ds(pl.multiple_of(c * ch, ch), ch)
+
+    def times_own(r, c):
+        return lax.dot_general(dall[r, :], wall[chunk(c), :], NT, preferred_element_type=f32)
+
+    def times_sent(d, k):
+        return lax.dot_general(d, wx[k].reshape(ch, qc + kvc), NT, preferred_element_type=f32)
+
+    summed = tok - held
+    last = kv_heads - 1
+
+    def sum_piece(slot, i):
+        at = (slot, pl.ds(i * BLOCK, BLOCK))
+        return remote(snd.at[at], rcv.at[at], rss.at[slot, i], rsr.at[slot, i], mp_dev(facing))
+
+    def out_piece(i):
+        at = block_rows(i)
+        return remote(tout.at[at], rin.at[at], tos.at[i], tor.at[i], mp_dev(partner))
+
+    early, late = slice(0, held), slice(held, tok)
+    cut = qc + kvc - pair
 
     leave = [pltpu.make_async_copy(ctx_ref, ctx_hbm, os.at[0])]
     leave[0].start()
@@ -798,19 +838,41 @@
     def _():
         dkv_out(0, True).wait_recv()
         dkv_across(1, 0).start()
+        for j, c in enumerate((facing_partner, facing, partner, z)):
+            part[j] = times_own(late, c)
+
+    @pl.when(outer)
+    def _():
+        tout[late, :] = times_own(late, partner).astype(bf16)
+        part[3] = times_own(late, z)
 
     finish_early(1)
-    pl.when(inner)(functools.partial(plane_pair, 0))
+
+    @pl.when(inner)
+    def _():
+        plane_start(2)
+        plane_pair(1)
+        part[4] = times_own(early, partner)
+        part[5] = times_own(early, z)
+
+    @pl.when(outer)
+    def _():
+        tout[early, :] = times_own(early, partner).astype(bf16)
+        part[5] = times_own(early, z)
+        dkv_out(last, False).wait_send()
+        dkv_out(last, True).wait_send()
+        for i in range(blocks):
+            out_piece(i).start()
 
     pw = gt.shape[3]
     gr_rows = pw * kv_heads
     dkvt = jnp.transpose(dall[:, qc:])
     for k in range(2):
-        part = (1 - core) if k == 0 else core
+        own_half = (1 - core) if k == 0 else core
 
         @pl.loop(0, chips)
         def _(j):
-            cols = pl.ds(pl.multiple_of((2 * j + part) * pw, pw), pw)
+            cols = pl.ds(pl.multiple_of((2 * j + own_half) * pw, pw), pw)
             prod = jnp.dot(dkvt, x_ref[:, cols], preferred_element_type=f32)
             if k == 0:
                 gt[0, j] = prod.astype(bf16)
@@ -821,49 +883,45 @@
             swap = remote(gt.at[0], sib, ss, sr, seq_dev(sibling))
             swap.start()
 
-    def chunk(c):
-        return pl.ds(pl.multiple_of(c * ch, ch), ch)
-
-    def times_own(r, c):
-        return lax.dot_general(dall[r, :], wall[chunk(c), :], NT, preferred_element_type=f32)
-
-    def times_sent(d, k):
-        return lax.dot_general(d, wx[k].reshape(ch, qc + kvc), NT, preferred_element_type=f32)
-
-    tile = 256 if ag % 2 == 0 else 128
-    summed = tok - held
-
-    def sum_piece(slot, i):
-        at = (slot, pl.ds(i * BLOCK, BLOCK))
-        return remote(snd.at[at], rcv.at[at], rss.at[slot, i], rsr.at[slot, i], mp_dev(facing))
-
-    def out_piece(i):
-        at = block_rows(i)
-        return remote(tout.at[at], rin.at[at], tos.at[i], tor.at[i], mp_dev(partner))
-
-    steps = tile // BLOCK
+    def times_cut(d, k):
+        return lax.dot_general(
+            d, wx[k, :, :, :, :cut].reshape(ch, cut), NT, preferred_element_type=f32)
+
+    def rest_on():
+        src = dx.at[1, :, pl.ds(cut, pair)]
+        return remote(src, src, fas.at[0], far.at[0], mp_dev(partner))
+
+    def rest_rows_on():
+        src = wx.at[3, :, :, :, pl.ds(cut, pair)]
+        return remote(src, src, fas.at[1], far.at[1], mp_dev(partner))
 
     @pl.when(inner)
     def _():
-        for g in range(kv_heads):
-            for b in range(ag, blocks):
-                dq_out(g, b).wait_recv()
+        for g in range(last):
             dkv_out(g, False).wait_recv()
         plane_done(0)
-        for slot in (1, 0):
-            c = facing_partner if slot == 1 else facing
-            for t in range(summed // tile):
-                r = slice(held + t * tile, held + (t + 1) * tile)
-                snd[slot, t * tile : (t + 1) * tile, :] = (
-                    times_own(r, c) + times_sent(dout[r, :], slot + 1)
-                ).astype(bf16)
-                for i in range(t * steps, (t + 1) * steps):
-                    sum_piece(slot, i).start()
-            if slot == 1:
-                dkv_out(1, True).wait_recv()
-                dkv_across(1, 1).start()
-                plane_relay(2)
-                plane_pair(1)
+        for b in range(ag, blocks):
+            for g in range(kv_heads):
+                dq_out(g, b).wait_recv()
+            i = b - ag
+            r = slice(b * BLOCK, (b + 1) * BLOCK)
+            snd[1, i * BLOCK : (i + 1) * BLOCK, :] = (
+                part[0, i * BLOCK : (i + 1) * BLOCK, :] + times_cut(dout[r, :cut], 1)
+            ).astype(bf16)
+            sum_piece(1, i).start()
+        plane_done(1)
+        rest_rows_on().start()
+        for which in range(2):
+            for g in range(kv_heads):
+                for b in range(ag):
+                    dq_across(which, g, b).wait_recv()
+                if which == 0 or g < last:
+                    dkv_across(which, g).wait_recv()
+        tout[early, :] = (
+            part[4] + times_sent(dx[0, early, :], 2) + times_cut(dx[1, early, :cut], 3)
+        ).astype(bf16)
+        for i in range(ag):
+            out_piece(i).start()
 
     swap.wait_recv()
 
@@ -882,11 +940,22 @@
 
     @pl.when(inner)
     def _():
+        plane_relay(2)
+        dkv_out(last, False).wait_recv()
+        dkv_rest_across(last).start()
+        dkv_out(last, True).wait_recv()
+        dkv_across(1, last).start()
+        snd[0] = (part[1] + times_sent(dout[late, :], 0)).astype(bf16)
+        for i in range(blocks - ag):
+            sum_piece(0, i).start()
+
+    @pl.when(inner)
+    def _():
         for i in range(summed // BLOCK):
             r = slice(held + i * BLOCK, held + (i + 1) * BLOCK)
-            own = times_own(r, partner)
+            p = slice(i * BLOCK, (i + 1) * BLOCK)
             sum_piece(1, i).wait_recv()
-            tout[r, :] = (own + rcv[1, i * BLOCK : (i + 1) * BLOCK, :].astype(f32)).astype(bf16)
+            tout[r, :] = (part[2, p, :] + rcv[1, p, :].astype(f32)).astype(bf16)
             out_piece(ag + i).start()
 
     for cp in sends:
@@ -906,30 +975,19 @@
         cp.start()
         sends.append(cp)
 
-    if ag:
-        @pl.when(inner)
-        def _():
-            for which in range(2):
-                for g in range(kv_heads):
-                    for b in range(ag):
-                        dq_across(which, g, b).wait_recv()
-                    dkv_across(which, g).wait_recv()
-            plane_pair(2)
-            plane_done(1)
-            plane_done(2)
-            for t in range(held // tile):
-                r = slice(t * tile, (t + 1) * tile)
-                tout[r, :] = (
-                    times_own(r, partner) + times_sent(dx[0, r, :], 4) + times_sent(dx[1, r, :], 6)
-                ).astype(bf16)
-                for i in range(t * steps, (t + 1) * steps):
-                    out_piece(i).start()
-            for t in range(held // tile):
-                r = slice(t * tile, (t + 1) * tile)
-                ig_ref[r, :] = (
-                    times_own(r, z) + times_sent(dout[r, :], 0)
-                    + times_sent(dx[0, r, :], 3) + times_sent(dx[1, r, :], 5)
-                ).astype(bf16)
+    @pl.when(inner)
+    def _():
+        dkv_across(1, last).wait_recv()
+        dkv_rest_across(last).wait_recv()
+        rest_on().start()
+        plane_pair(2)
+        plane_done(2)
+        for i in range(ag):
+            out_piece(i).wait_recv()
+        ig_ref[early, :] = (
+            part[5] + rin[early, :].astype(f32)
+            + times_sent(dx[0, early, :], 4) + times_sent(dx[1, early, :], 5)
+        ).astype(bf16)
 
     got[0] = piece[...]
     for cp in sends:
@@ -951,31 +1009,30 @@
 
     @pl.when(inner)
     def _():
-        for t in range(summed // tile):
-            for i in range(t * steps, (t + 1) * steps):
-                sum_piece(0, i).wait_recv()
-            r = slice(held + t * tile, held + (t + 1) * tile)
-            ig_ref[r, :] = (
-                times_own(r, z) + times_sent(dout[r, :], 0)
-                + rcv[0, t * tile : (t + 1) * tile, :].astype(f32)
-            ).astype(bf16)
+        for i in range(ag, blocks):
+            out_piece(i).wait_recv()
+        for i in range(summed // BLOCK):
+            sum_piece(0, i).wait_recv()
+        ig_ref[late, :] = (part[3] + rin[late, :].astype(f32) + rcv[0].astype(f32)).astype(bf16)
 
     @pl.when(outer)
     def _():
-        order = list(range(ag, blocks)) + list(range(ag))
-        for i in order:
-            r = slice(i * BLOCK, (i + 1) * BLOCK)
-            own = times_own(r, z)
+        rest_rows_on().wait_recv()
+        for i in range(blocks):
             out_piece(i).wait_recv()
-            ig_ref[r, :] = (own + rin[r, :].astype(f32)).astype(bf16)
+        rest_on().wait_recv()
+        for r, mine_part in ((early, part[5]), (late, part[3])):
+            far_part = lax.dot_general(
+                dx[1, r, cut:], wx[3, :, :, :, cut:].reshape(ch, pair), NT, preferred_element_type=f32)
+            ig_ref[r, :] = (mine_part + far_part + rin[r, :].astype(f32)).astype(bf16)
 
     @pl.when(outer)
     def _():
         for g in range(kv_heads):
             for b in range(blocks):
                 dq_out(g, b).wait_send()
-            dkv_out(g, False).wait_send()
-            if ag:
+            if g < last:
+                dkv_out(g, False).wait_send()
                 dkv_out(g, True).wait_send()
         each(zh[0], "wait_send")
         each(zh[1], "wait_send")
@@ -987,16 +1044,19 @@
                 for b in range(ag):
                     dq_across(which, g, b).wait_send()
                 dkv_across(which, g).wait_send()
+        dkv_rest_across(last).wait_send()
+        rest_on().wait_send()
+        rest_rows_on().wait_send()
         for slot in range(2):
             for i in range(blocks - ag):
                 sum_piece(slot, i).wait_send()
-        for i in range(blocks):
-            out_piece(i).wait_send()
         for group in za:
             each(group, "wait_send")
         for group in (to_x, to_y, via_x, via_y, *to_sib):
             each(group, "wait_send")
 
+    for i in range(blocks):
+        out_piece(i).wait_send()
     for cp in leave:
         cp.wait()
     pl.when(has_left)(kv_left.wait_send)
@@ -1132,13 +1192,14 @@
         vmem((2, kv_heads, MARGIN, pair), bf16),
         vmem((2, kv_heads, MARGIN, pair), bf16),
         vmem((tok, qc + kvc), bf16),
-        vmem((7 if ag else 3, max(chips, 1), 2, max(ch // n, 8), qc + kvc), bf16),
+        vmem((6, max(chips, 1), 2, max(ch // n, 8), qc + kvc), bf16),
         vmem((tok, qc + kvc), bf16),
-        vmem((2, max(held, BLOCK), qc + kvc), bf16),
+        vmem((2, tok, qc + kvc), bf16),
         vmem((2, max(tok - held, BLOCK), ch), bf16),
         vmem((2, max(tok - held, BLOCK), ch), bf16),
         vmem((tok, ch), bf16),
         vmem((tok, ch), bf16),
+        vmem((6, MARGIN, ch), f32),
         vmem((2, chips, kvc, pw), bf16),
         vmem((chips, kvc, pw), f32),
         vmem((chips, kvc, pw), bf16),
@@ -1156,16 +1217,17 @@
         dma((2, kv_heads)),
         dma, dma, dma((chips,)), dma((chips,)), dma((chips,)), dma((chips,)), dma, dma,
         dma((2, 3)), dma((2, 3)),
-        dma((3, 2)), dma((3, 2)),
+        dma((4, 2)), dma((4, 2)),
         dma((2, 3)), dma((2, 3)),
         dma((2, 3)), dma((2, 3)),
         dma((3, 4)), dma((3, 4)),
         dma((kv_heads, blocks)), dma((kv_heads, blocks)),
         dma((kv_heads, 2)), dma((kv_heads, 2)),
         dma((2, kv_heads, blocks)), dma((2, kv_heads, blocks)),
-        dma((2, kv_heads)), dma((2, kv_heads)),
+        dma((3, kv_heads)), dma((3, kv_heads)),
         dma((2, blocks)), dma((2, blocks)),
         dma((blocks,)), dma((blocks,)),
+        dma((2,)), dma((2,)),
     ]
     if relay:
         scratch = relay_scratch

time: 65.3 us -> 57.3 us (0.88)
  Pallas kernels: 64.4 us -> 56.1 us
    pallas_call x1, Pallas kernels: 61.7 us -> 53.4 us  [local(): pl.pallas_call(body, out_shape=[jax.ShapeDtypeStruct((tok, qc), bf16), ja...]
where the time goes in v2:
time: 57.3 us; the launch traced here: 56.8 us
  Pallas kernels  56.1 us (98%)
  between operations  0.64 us (1%)
    pallas_call x1, Pallas kernels, local(): pl.pallas_call(body, out_shape=[jax.ShapeDtypeStruct((tok, qc), bf16), ja...  53.4 us
    pallas_call x1, Pallas kernels, written(): pl.pallas_call(write_kernel, out_shape=[jax.ShapeDtypeStruct(a.shape, t)...  2.75 us

profile of v2, /device:TPU:0, one launch (start us, length us, event | category | flops | bytes accessed | tf_op | source)
XLA Modules:
  0.0 56.8 jit_solution(6875298071249076395)
XLA Ops:
  0.6 53.4 %fused.1 = (bf16[512,512]{1,0:T(8,128)(2,1)}, bf16[512,512]{1,0:T(8,128)(2,1)}, bf16[4096,128]{1,0:T(8,128)(2,1)}) custom-call(bf16[512,2048]{1,0:T(8,128)(2,1)} %x_hbm.1, bf16[512,2048]{1,0:T(8,128)(2,1)} %oc_hbm.1, bf16[2048,512]{1,0:T(8,128)(2,1)} %wq_hbm.1, bf16[4096,128]{1,0:T(8,128)(2,1)} %bitcast.3, bf16[512,2048]{1,0:T(8,128)(2,1)} %wo_hbm.1, ...), custom_call_target="tpu_custom_call" | custom-call | tf_op jit(solution)/shard_map/fused/pallas_call | solution.py:1237
  54.0 2.7 %write.1 = (bf16[512,512]{1,0:T(8,128)(2,1)}, bf16[512,512]{1,0:T(8,128)(2,1)}, f32[4096,128]{1,0:T(8,128)}) custom-call(bf16[512,512]{1,0:T(8,128)(2,1)} %get-tuple-element.9.ctx_hbm, bf16[512,512]{1,0:T(8,128)(2,1)} %get-tuple-element.10.ig_hbm, bf16[4096,128]{1,0:T(8,128)(2,1)} %get-tuple-element.11.kvg_hbm), custom_call_target="tpu_custom_call" | custom-call | tf_op jit(solution)/shard_map/write/pallas_call | solution.py:1094

commit v3 on v2

--- a/solution.py
+++ b/solution.py
@@ -425,10 +425,10 @@
 
 
 def relay_kernel(n, ag, x_hbm, oc_hbm, wq_hbm, wkv_hbm, wo_hbm, seg_ref, band_ref,
-                 ctx_hbm, ig_ref, kvg_hbm, ctx_ref, raw, wide_raw, x_ref, oc_ref, wall, wo_ref, q_ref, dc_ref,
+                 ctx_ref, ig_ref, kvg_ref, raw, wide_raw, x_ref, oc_ref, wall, wo_ref, q_ref, dc_ref,
                  kvx, kdocs, bias, grad, halo, hin, dall, wx, dout, dx, snd, rcv, tout, rin, part,
                  gt, gsum, sib, quart, got, mine, mix, piece, sib2,
-                 ls, os, ks, kr, hs, hr, ss, sr, qs, qr, gs, gr, fs, fr,
+                 ls, ks, kr, hs, hr, ss, sr, qs, qr, gs, gr, fs, fr,
                  zhs, zhr, zas, zar, pls, plr, pfs, pfr, pss, psr,
                  oqs, oqr, oks, okr, xqs, xqr, xks, xkr, rss, rsr, tos, tor, fas, far):
     tok, qc = q_ref.shape
@@ -736,8 +736,7 @@
         cols = slice(g * wide, (g + 1) * wide)
         kcols = slice(g * pair, (g + 1) * pair)
 
-        @pl.loop(0, blocks)
-        def _(b):
+        def attend(b):
             first = pl.multiple_of(b * BLOCK, BLOCK)
             qt = side_by_side(jnp.transpose(q_ref[pl.ds(first, BLOCK), cols] * SCALE))
             dct = side_by_side(jnp.transpose(dc_ref[pl.ds(first, BLOCK), cols]))
@@ -762,48 +761,49 @@
             d_kv = d_kv + lax.dot_general(wh, dcz, NT, preferred_element_type=f32)
             grad[pl.ds(first, WINDOW), kcols] += d_kv
 
+        @pl.loop(0, blocks // 2)
+        def _(pair_index):
+            for b in (2 * pair_index, 2 * pair_index + 1):
+                attend(b)
+
+            first_pair = pair_index == 0
+
             @pl.when(outer)
             def _():
-                dq_out(g, b).start()
-
-            @pl.when(inner & (b < ag))
-            def _():
-                dq_across(0, g, b).start()
-
-            @pl.when(inner & (b >= 2) & (b < ag + 2))
-            def _():
-                dq_out(g, b - 2).wait_recv()
-                dq_across(1, g, b - 2).start()
-
-            @pl.when(b == 1)
+                for b in (2 * pair_index, 2 * pair_index + 1):
+                    dq_out(g, b).start()
+
+            @pl.when(first_pair)
             def _():
                 halo[0, g] = grad[:MARGIN, kcols].astype(bf16)
                 pl.when(has_left)(halo_left(g).start)
 
-            if g == 0:
-                @pl.when(inner & (b == 1))
-                def _():
+            @pl.when(inner & first_pair)
+            def _():
+                for b in range(2):
+                    dq_across(0, g, b).start()
+                if g == 0:
                     each(za[0] + za[1] + za[2] + za[3], "wait_recv")
                     plane_start(1)
-
-                @pl.when(inner & (b == blocks - 1))
-                def _():
+                if g == 1:
+                    plane_relay(1)
+
+            @pl.when(inner & jnp.logical_not(first_pair))
+            def _():
+                for b in range(2):
+                    dq_out(g, b).wait_recv()
+                    dq_across(1, g, b).start()
+                if g == 0:
                     plane_relay(0)
+                if g == 1:
+                    plane_pair(0)
 
             if g == 1:
-                @pl.when(inner & (b == 1))
-                def _():
-                    plane_relay(1)
-
-                @pl.when(b == 1)
+                @pl.when(first_pair)
                 def _():
                     finish_early(0)
                     finish_late(0)
 
-                @pl.when(inner & (b == blocks - 1))
-                def _():
-                    plane_pair(0)
-
         halo[1, g] = grad[MARGIN + tok :, kcols].astype(bf16)
         pl.when(has_right)(halo_right(g).start)
 
@@ -830,8 +830,6 @@
     early, late = slice(0, held), slice(held, tok)
     cut = qc + kvc - pair
 
-    leave = [pltpu.make_async_copy(ctx_ref, ctx_hbm, os.at[0])]
-    leave[0].start()
     finish_late(1)
 
     @pl.when(inner)
@@ -996,15 +994,11 @@
     swap.start()
     for k in range(chips):
         src = (chip + chips - k) % chips
-        rows = pl.ds(pl.multiple_of((2 * src + core) * gr_rows, gr_rows), gr_rows)
-        leave.append(pltpu.make_async_copy(got.at[k], kvg_hbm.at[rows], os.at[1 + k]))
-        leave[-1].start()
+        kvg_ref[pl.ds(pl.multiple_of((2 * src + core) * gr_rows, gr_rows), gr_rows), :] = got[k]
     swap.wait_recv()
     for k in range(chips):
         src = (chip + chips - k) % chips
-        rows = pl.ds(pl.multiple_of((2 * src + 1 - core) * gr_rows, gr_rows), gr_rows)
-        leave.append(pltpu.make_async_copy(sib2.at[k], kvg_hbm.at[rows], os.at[1 + chips + k]))
-        leave[-1].start()
+        kvg_ref[pl.ds(pl.multiple_of((2 * src + 1 - core) * gr_rows, gr_rows), gr_rows), :] = sib2[k]
     swap.wait_send()
 
     @pl.when(inner)
@@ -1057,8 +1051,6 @@
 
     for i in range(blocks):
         out_piece(i).wait_send()
-    for cp in leave:
-        cp.wait()
     pl.when(has_left)(kv_left.wait_send)
     pl.when(has_right)(kv_right.wait_send)
     for g in range(kv_heads):
@@ -1086,6 +1078,41 @@
         stores[i].start()
     for cp in stores:
         cp.wait()
+
+
+def store_kernel(ctx_ref, ig_ref, kvg_ref, ctx_out, ig_out, kvg_out, full, outs):
+    pieces, rows = full.shape[0], full.shape[1]
+    stores = [
+        pltpu.make_async_copy(ctx_ref, ctx_out, outs.at[pieces]),
+        pltpu.make_async_copy(ig_ref, ig_out, outs.at[pieces + 1]),
+    ]
+    for cp in stores:
+        cp.start()
+    for i in range(pieces):
+        full[i] = kvg_ref[i * rows : (i + 1) * rows, :].astype(f32)
+        stores.append(pltpu.make_async_copy(full.at[i], kvg_out.at[pl.ds(i * rows, rows)], outs.at[i]))
+        stores[-1].start()
+    for cp in stores:
+        cp.wait()
+
+
+def stored(*arrays):
+    pieces = 8
+    rows, lanes = arrays[2].shape[0] // pieces, arrays[2].shape[1]
+    return pl.pallas_call(
+        store_kernel,
+        out_shape=[
+            jax.ShapeDtypeStruct(a.shape, t) for a, t in zip(arrays, (bf16, bf16, f32))
+        ],
+        in_specs=[VMEM] * 3,
+        out_specs=[ANY] * 3,
+        scratch_shapes=[
+            pltpu.VMEM((pieces, rows, lanes), f32),
+            pltpu.SemaphoreType.DMA((pieces + 2,)),
+        ],
+        compiler_params=pltpu.CompilerParams(vmem_limit_bytes=30 * 2**20),
+        name="store",
+    )(*arrays)
 
 
 def written(*arrays):
@@ -1176,7 +1203,6 @@
     ag = AHEAD
     held = ag * BLOCK
     relay_scratch = [
-        vmem((tok, qc), bf16),
         vmem((width * kv_heads, pair), bf16),
         vmem((256 * kv_heads, pair), f32),
         vmem((tok, width), bf16),
@@ -1210,46 +1236,51 @@
         vmem((pw * kv_heads, pair), bf16),
         vmem((chips, pw * kv_heads, pair), bf16),
         dma((5,)),
-        dma((1 + n,)),
         dma((2,)),
         dma((2,)),
         dma((2, kv_heads)),
         dma((2, kv_heads)),
         dma, dma, dma((chips,)), dma((chips,)), dma((chips,)), dma((chips,)), dma, dma,
-        dma((2, 3)), dma((2, 3)),
+        dma((2, 2)), dma((2, 2)),
         dma((4, 2)), dma((4, 2)),
         dma((2, 3)), dma((2, 3)),
         dma((2, 3)), dma((2, 3)),
         dma((3, 4)), dma((3, 4)),
         dma((kv_heads, blocks)), dma((kv_heads, blocks)),
         dma((kv_heads, 2)), dma((kv_heads, 2)),
-        dma((2, kv_heads, blocks)), dma((2, kv_heads, blocks)),
+        dma((2, kv_heads, ag)), dma((2, kv_heads, ag)),
         dma((3, kv_heads)), dma((3, kv_heads)),
-        dma((2, blocks)), dma((2, blocks)),
+        dma((2, blocks - ag)), dma((2, blocks - ag)),
         dma((blocks,)), dma((blocks,)),
         dma((2,)), dma((2,)),
     ]
     if relay:
         scratch = relay_scratch
         body = functools.partial(relay_kernel, n, ag)
+        shapes = [vmem((tok, qc), bf16), vmem((tok, ch), bf16), vmem(kvg_shape, bf16)]
+        out_specs = [VMEM] * 3
     else:
         body = functools.partial(fused_kernel, n, m, sum_seq)
-    context, input_grad, other = pl.pallas_call(
-        body,
-        out_shape=[
+        shapes = [
             jax.ShapeDtypeStruct((tok, qc), bf16),
             jax.ShapeDtypeStruct((tok, ch), bf16),
             jax.ShapeDtypeStruct(kvg_shape, bf16),
-        ],
+        ]
+        out_specs = [ANY, VMEM, ANY]
+    context, input_grad, other = pl.pallas_call(
+        body,
+        out_shape=shapes,
         in_specs=[ANY] * 5 + [VMEM, SMEM],
-        out_specs=[ANY, VMEM, ANY],
+        out_specs=out_specs,
         scratch_shapes=scratch,
         compiler_params=pltpu.CompilerParams(
             vmem_limit_bytes=56 * 2**20, collective_id=0, has_side_effects=True
         ),
         name="fused",
     )(normed, out_cotangent, query_weight, wkv, out_weight, segments.reshape(-1, BLOCK), band_mask)
-    if sum_seq:
+    if relay:
+        context, input_grad, kv_grad = stored(context, input_grad, other)
+    elif sum_seq:
         context, input_grad, kv_grad = written(context, input_grad, other)
     else:
         kv_grad = lax.dot_general(normed, other, (((0,), (0,)), ((), ())), preferred_element_type=f32)

time: 57.3 us -> 55.2 us (0.963)
  Pallas kernels: 56.1 us -> 54.3 us
    pallas_call x2, Pallas kernels: 56.1 us -> 54.3 us  [the longest x1 52.6 us: local(): pl.pallas_call(body, out_shape=shapes, in_specs=[ANY] * 5 + [VMEM, SMEM],...]
where the time goes in v3:
time: 55.2 us; the launch traced here: 55 us
  Pallas kernels  54.3 us (98%)
  between operations  0.64 us (1%)
    pallas_call x1, Pallas kernels, local(): pl.pallas_call(body, out_shape=shapes, in_specs=[ANY] * 5 + [VMEM, SMEM],...  52.6 us
    pallas_call x1, Pallas kernels, stored(): pl.pallas_call(store_kernel, out_shape=[jax.ShapeDtypeStruct(a.shape, t)...  1.74 us

profile of v3, /device:TPU:0, one launch (start us, length us, event | category | flops | bytes accessed | tf_op | source)
XLA Modules:
  0.0 55.0 jit_solution(6153043755103470896)
XLA Ops:
  0.6 52.6 %fused.1 = (bf16[512,512]{1,0:T(8,128)(2,1)S(1)}, bf16[512,512]{1,0:T(8,128)(2,1)S(1)}, bf16[4096,128]{1,0:T(8,128)(2,1)S(1)}) custom-call(bf16[512,2048]{1,0:T(8,128)(2,1)} %x_hbm.1, bf16[512,2048]{1,0:T(8,128)(2,1)} %oc_hbm.1, bf16[2048,512]{1,0:T(8,128)(2,1)} %wq_hbm.1, bf16[4096,128]{1,0:T(8,128)(2,1)} %bitcast.3, bf16[512,2048]{1,0:T(8,128)(2,1)} %wo_hbm.1, ...), custom_call_target="tpu_custom_call" | custom-call | tf_op jit(solution)/shard_map/fused/pallas_call | solution.py:1270
  53.2 1.7 %store.1 = (bf16[512,512]{1,0:T(8,128)(2,1)}, bf16[512,512]{1,0:T(8,128)(2,1)}, f32[4096,128]{1,0:T(8,128)}) custom-call(bf16[512,512]{1,0:T(8,128)(2,1)S(1)} %get-tuple-element.9.ctx_ref, bf16[512,512]{1,0:T(8,128)(2,1)S(1)} %get-tuple-element.10.ig_ref, bf16[4096,128]{1,0:T(8,128)(2,1)S(1)} %get-tuple-element.11.kvg_ref), custom_call_target="tpu_custom_call" | custom-call | tf_op jit(solution)/shard_map/store/pallas_call | solution.py:1102

commit v4 on v3

--- a/solution.py
+++ b/solution.py
@@ -708,7 +708,7 @@
         return remote(src, dx.at[(which,) + at], xks.at[which, g], xkr.at[which, g], mp_dev(facing))
 
     def dkv_rest_across(g):
-        at = (pl.ds(held, tok - held), dkv_cols(g))
+        at = (pl.ds(held, BLOCK), dkv_cols(g))
         return remote(dout.at[at], dx.at[(1,) + at], xks.at[2, g], xkr.at[2, g], mp_dev(facing))
 
     def halo_left(g):
@@ -881,12 +881,27 @@
             swap = remote(gt.at[0], sib, ss, sr, seq_dev(sibling))
             swap.start()
 
+    swap.wait_recv()
+
+    def other(k):
+        return (chip + k) % chips
+
+    sends = []
+    for k in range(1, chips):
+        j = other(k)
+        gt[1, j] = (gsum[j] + sib[j].astype(f32)).astype(bf16)
+        cp = remote(gt.at[1, j], quart.at[k], qs.at[k], qr.at[k], seq_dev(j * 2 + core))
+        cp.start()
+        sends.append(cp)
+    mine[...] = gsum[chip] + sib[chip].astype(f32)
+    swap.wait_send()
+
     def times_cut(d, k):
         return lax.dot_general(
             d, wx[k, :, :, :, :cut].reshape(ch, cut), NT, preferred_element_type=f32)
 
     def rest_on():
-        src = dx.at[1, :, pl.ds(cut, pair)]
+        src = dx.at[1, pl.ds(0, held + BLOCK), pl.ds(cut, pair)]
         return remote(src, src, fas.at[0], far.at[0], mp_dev(partner))
 
     def rest_rows_on():
@@ -898,7 +913,7 @@
         for g in range(last):
             dkv_out(g, False).wait_recv()
         plane_done(0)
-        for b in range(ag, blocks):
+        for b in range(ag, ag + 1):
             for g in range(kv_heads):
                 dq_out(g, b).wait_recv()
             i = b - ag
@@ -921,25 +936,20 @@
         for i in range(ag):
             out_piece(i).start()
 
-    swap.wait_recv()
-
-    def other(k):
-        return (chip + k) % chips
-
-    sends = []
-    for k in range(1, chips):
-        j = other(k)
-        gt[1, j] = (gsum[j] + sib[j].astype(f32)).astype(bf16)
-        cp = remote(gt.at[1, j], quart.at[k], qs.at[k], qr.at[k], seq_dev(j * 2 + core))
-        cp.start()
-        sends.append(cp)
-    mine[...] = gsum[chip] + sib[chip].astype(f32)
-    swap.wait_send()
-
     @pl.when(inner)
     def _():
         plane_relay(2)
+        for b in range(ag + 1, blocks):
+            for g in range(kv_heads):
+                dq_out(g, b).wait_recv()
         dkv_out(last, False).wait_recv()
+        for b in range(ag + 1, blocks):
+            i = b - ag
+            r = slice(b * BLOCK, (b + 1) * BLOCK)
+            snd[1, i * BLOCK : (i + 1) * BLOCK, :] = (
+                part[0, i * BLOCK : (i + 1) * BLOCK, :] + times_sent(dout[r, :], 1)
+            ).astype(bf16)
+            sum_piece(1, i).start()
         dkv_rest_across(last).start()
         dkv_out(last, True).wait_recv()
         dkv_across(1, last).start()
@@ -988,18 +998,20 @@
         ).astype(bf16)
 
     got[0] = piece[...]
-    for cp in sends:
-        cp.wait()
-    swap = remote(got, sib2, fs, fr, seq_dev(sibling))
-    swap.start()
-    for k in range(chips):
-        src = (chip + chips - k) % chips
-        kvg_ref[pl.ds(pl.multiple_of((2 * src + core) * gr_rows, gr_rows), gr_rows), :] = got[k]
-    swap.wait_recv()
-    for k in range(chips):
-        src = (chip + chips - k) % chips
-        kvg_ref[pl.ds(pl.multiple_of((2 * src + 1 - core) * gr_rows, gr_rows), gr_rows), :] = sib2[k]
-    swap.wait_send()
+    swaps = []
+    for j in range(chips):
+        if j:
+            sends[j - 1].wait()
+        swaps.append(remote(got.at[j], sib2.at[j], fs.at[j], fr.at[j], seq_dev(sibling)))
+        swaps[-1].start()
+        src = (chip + chips - j) % chips
+        kvg_ref[pl.ds(pl.multiple_of((2 * src + core) * gr_rows, gr_rows), gr_rows), :] = got[j]
+    for j in range(chips):
+        swaps[j].wait_recv()
+        src = (chip + chips - j) % chips
+        kvg_ref[pl.ds(pl.multiple_of((2 * src + 1 - core) * gr_rows, gr_rows), gr_rows), :] = sib2[j]
+    for cp in swaps:
+        cp.wait_send()
 
     @pl.when(inner)
     def _():
@@ -1015,7 +1027,9 @@
         for i in range(blocks):
             out_piece(i).wait_recv()
         rest_on().wait_recv()
-        for r, mine_part in ((early, part[5]), (late, part[3])):
+        tail = slice(held + BLOCK, tok)
+        ig_ref[tail, :] = (part[3, BLOCK:, :] + rin[tail, :].astype(f32)).astype(bf16)
+        for r, mine_part in ((early, part[5]), (slice(held, held + BLOCK), part[3, :BLOCK, :])):
             far_part = lax.dot_general(
                 dx[1, r, cut:], wx[3, :, :, :, cut:].reshape(ch, pair), NT, preferred_element_type=f32)
             ig_ref[r, :] = (mine_part + far_part + rin[r, :].astype(f32)).astype(bf16)
@@ -1240,7 +1254,7 @@
         dma((2,)),
         dma((2, kv_heads)),
         dma((2, kv_heads)),
-        dma, dma, dma((chips,)), dma((chips,)), dma((chips,)), dma((chips,)), dma, dma,
+        dma, dma, dma((chips,)), dma((chips,)), dma((chips,)), dma((chips,)), dma((chips,)), dma((chips,)),
         dma((2, 2)), dma((2, 2)),
         dma((4, 2)), dma((4, 2)),
         dma((2, 3)), dma((2, 3)),

time: 55.2 us -> 54.8 us (level)
  no operation moved by 1% of the time
where the time goes in v4:
time: 54.8 us; the launch traced here: 54.5 us
  Pallas kernels  53.9 us (98%)
  between operations  0.64 us (1%)
    pallas_call x1, Pallas kernels, local(): pl.pallas_call(body, out_shape=shapes, in_specs=[ANY] * 5 + [VMEM, SMEM],...  52.2 us
    pallas_call x1, Pallas kernels, stored(): pl.pallas_call(store_kernel, out_shape=[jax.ShapeDtypeStruct(a.shape, t)...  1.74 us

profile of v4, /device:TPU:0, one launch (start us, length us, event | category | flops | bytes accessed | tf_op | source)
XLA Modules:
  0.0 54.5 jit_solution(13721465824844684796)
XLA Ops:
  0.6 52.2 %fused.1 = (bf16[512,512]{1,0:T(8,128)(2,1)S(1)}, bf16[512,512]{1,0:T(8,128)(2,1)S(1)}, bf16[4096,128]{1,0:T(8,128)(2,1)S(1)}) custom-call(bf16[512,2048]{1,0:T(8,128)(2,1)} %x_hbm.1, bf16[512,2048]{1,0:T(8,128)(2,1)} %oc_hbm.1, bf16[2048,512]{1,0:T(8,128)(2,1)} %wq_hbm.1, bf16[4096,128]{1,0:T(8,128)(2,1)} %bitcast.3, bf16[512,2048]{1,0:T(8,128)(2,1)} %wo_hbm.1, ...), custom_call_target="tpu_custom_call" | custom-call | tf_op jit(solution)/shard_map/fused/pallas_call | solution.py:1284
  52.8 1.7 %store.1 = (bf16[512,512]{1,0:T(8,128)(2,1)}, bf16[512,512]{1,0:T(8,128)(2,1)}, f32[4096,128]{1,0:T(8,128)}) custom-call(bf16[512,512]{1,0:T(8,128)(2,1)S(1)} %get-tuple-element.9.ctx_ref, bf16[512,512]{1,0:T(8,128)(2,1)S(1)} %get-tuple-element.10.ig_ref, bf16[4096,128]{1,0:T(8,128)(2,1)S(1)} %get-tuple-element.11.kvg_ref), custom_call_target="tpu_custom_call" | custom-call | tf_op jit(solution)/shard_map/store/pallas_call | solution.py:1116

commit v5 on v4

--- a/solution.py
+++ b/solution.py
@@ -836,13 +836,11 @@
     def _():
         dkv_out(0, True).wait_recv()
         dkv_across(1, 0).start()
-        for j, c in enumerate((facing_partner, facing, partner, z)):
-            part[j] = times_own(late, c)
+        part[0] = times_own(late, facing_partner)
 
     @pl.when(outer)
     def _():
         tout[late, :] = times_own(late, partner).astype(bf16)
-        part[3] = times_own(late, z)
 
     finish_early(1)
 
@@ -851,11 +849,11 @@
         plane_start(2)
         plane_pair(1)
         part[4] = times_own(early, partner)
-        part[5] = times_own(early, z)
 
     @pl.when(outer)
     def _():
         tout[early, :] = times_own(early, partner).astype(bf16)
+        part[3] = times_own(late, z)
         part[5] = times_own(early, z)
         dkv_out(last, False).wait_send()
         dkv_out(last, True).wait_send()
@@ -938,6 +936,9 @@
 
     @pl.when(inner)
     def _():
+        for j, c in ((1, facing), (2, partner), (3, z)):
+            part[j] = times_own(late, c)
+        part[5] = times_own(early, z)
         plane_relay(2)
         for b in range(ag + 1, blocks):
             for g in range(kv_heads):
@@ -1111,7 +1112,7 @@
 
 
 def stored(*arrays):
-    pieces = 8
+    pieces = 4
     rows, lanes = arrays[2].shape[0] // pieces, arrays[2].shape[1]
     return pl.pallas_call(
         store_kernel,

time: 54.8 us -> 54.7 us (level)
  no operation moved by 1% of the time
where the time goes in v5:
time: 54.7 us; the launch traced here: 54.4 us
  Pallas kernels  53.8 us (98%)
  between operations  0.64 us (1%)
    pallas_call x1, Pallas kernels, local(): pl.pallas_call(body, out_shape=shapes, in_specs=[ANY] * 5 + [VMEM, SMEM],...  52.1 us
    pallas_call x1, Pallas kernels, stored(): pl.pallas_call(store_kernel, out_shape=[jax.ShapeDtypeStruct(a.shape, t)...  1.71 us

profile of v5, /device:TPU:0, one launch (start us, length us, event | category | flops | bytes accessed | tf_op | source)
XLA Modules:
  0.0 54.4 jit_solution(15313762019601831303)
XLA Ops:
  0.6 52.1 %fused.1 = (bf16[512,512]{1,0:T(8,128)(2,1)S(1)}, bf16[512,512]{1,0:T(8,128)(2,1)S(1)}, bf16[4096,128]{1,0:T(8,128)(2,1)S(1)}) custom-call(bf16[512,2048]{1,0:T(8,128)(2,1)} %x_hbm.1, bf16[512,2048]{1,0:T(8,128)(2,1)} %oc_hbm.1, bf16[2048,512]{1,0:T(8,128)(2,1)} %wq_hbm.1, bf16[4096,128]{1,0:T(8,128)(2,1)} %bitcast.3, bf16[512,2048]{1,0:T(8,128)(2,1)} %wo_hbm.1, ...), custom_call_target="tpu_custom_call" | custom-call | tf_op jit(solution)/shard_map/fused/pallas_call | solution.py:1285
  52.7 1.7 %store.1 = (bf16[512,512]{1,0:T(8,128)(2,1)}, bf16[512,512]{1,0:T(8,128)(2,1)}, f32[4096,128]{1,0:T(8,128)}) custom-call(bf16[512,512]{1,0:T(8,128)(2,1)S(1)} %get-tuple-element.9.ctx_ref, bf16[512,512]{1,0:T(8,128)(2,1)S(1)} %get-tuple-element.10.ig_ref, bf16[4096,128]{1,0:T(8,128)(2,1)S(1)} %get-tuple-element.11.kvg_ref), custom_call_target="tpu_custom_call" | custom-call | tf_op jit(solution)/shard_map/store/pallas_call | solution.py:1117
